TPU v7x, 128 devices: a whole 4x4x4 slice. The times are simulated.
128 devices in a mesh: lon: 32 (over z_lo, y, x), lat: 4 (over z_hi, core).
Axes of the slice: x: 4, y: 4, z: 4 (z_hi: 2, z_lo: 2; z = z_hi * 2 + z_lo), core: 2. Of those that a mesh axis runs over, the one named last changes fastest.
Arguments:
- fields: bfloat16 [256, 128, 512], P('lon', 'lat'), may hold values from -6 to 6
- cotangent: bfloat16 [256, 128, 512], P('lon', 'lat'), may hold values from -16 to 16
- surface: int32 [256, 128], replicated, may hold values from 0 to 2
- qkv_weight: bfloat16 [2, 512, 1536], replicated, may hold values from -0.25 to 0.25
- proj_weight: bfloat16 [2, 512, 512], replicated, may hold values from -2 to 2
- norm_gain: float32 [2, 512], replicated, may hold values from 0.25 to 1.75
- log_scale: float32 [2, 16], replicated, may hold values from 1.4 to 3.4
- pos_table: float32 [2, 16, 64, 64], replicated, may hold values from -4 to 4
Outputs:
- d_fields: bfloat16 [256, 128, 512], P('lon', 'lat')
- d_qkv_weight: float32 [2, 512, 1536], P(None, ('lon', 'lat'))
- d_proj_weight: float32 [2, 512, 512], P(None, ('lon', 'lat'))
- d_norm_gain: float32 [2, 512], replicated
- d_log_scale: float32 [2, 16], replicated
- d_pos_table: float32 [2, 16, 64, 64], replicated
All inputs are finite; a program needn't handle non-finite values.
Results may differ from a plain program's by a relative error of at most 0.03.
The roundings to bfloat16 on the way count: a program that leaves them out, or rounds other values in their place, can miss the bound.
Values may be sent and summed in bfloat16 or wider, within the bound.
A program may use at most 128 MiB of HBM per device.

v0:
```python
import math

import jax
import jax.numpy as jnp
from jax import lax
from jax.sharding import PartitionSpec as P

WIN = 8


NORM_EPS = 1e-06
LAYER_EPS = 1e-05
BIAS_CAP = 16.0


def passed_along(block, axis, distance):
    devices = range(lax.axis_size(axis))
    route = [((i - distance) % len(devices), i) for i in devices]
    return lax.ppermute(block, axis, route)


def to_windows(tile):
    rest = tile.shape[2:]
    lon_cells = tile.shape[0]
    lat_cells = tile.shape[1]
    grid = tile.reshape((lon_cells // WIN, WIN, lat_cells // WIN, WIN) + rest)
    grid = jnp.swapaxes(grid, 1, 2)
    return grid.reshape((-1, WIN * WIN) + rest)


def from_windows(blocks, lon_cells, lat_cells):
    rest = blocks.shape[2:]
    grid = blocks.reshape((lon_cells // WIN, lat_cells // WIN, WIN, WIN) + rest)
    grid = jnp.swapaxes(grid, 1, 2)
    return grid.reshape((lon_cells, lat_cells) + rest)


def pair_mask(labels):
    return labels[:, :, None] == labels[:, None, :]


def roll_lon(stack, direction, margin):
    piece = stack[:, :margin] if direction < 0 else stack[:, -margin:]
    arrived = passed_along(piece, "lon", direction)
    if direction < 0:
        return jnp.concatenate([stack[:, margin:], arrived], axis=1)
    return jnp.concatenate([arrived, stack[:, :-margin]], axis=1)


def roll_lat(stack, direction, margin):
    piece = stack[:, :, :margin] if direction < 0 else stack[:, :, -margin:]
    arrived = passed_along(piece, "lat", direction)
    if direction < 0:
        return jnp.concatenate([stack[:, :, margin:], arrived], axis=2)
    return jnp.concatenate([arrived, stack[:, :, :-margin]], axis=2)


def attend_forward(tokens, allowed, w_inner, w_outer, gain, log_gain, table):
    count, length, width = tokens.shape
    heads = log_gain.shape[0]
    depth = width // heads
    flat = tokens.reshape(count * length, width)
    mixed = jnp.dot(flat, w_inner, preferred_element_type=jnp.float32)
    mixed = mixed.reshape(count, length, 3, heads, depth)
    query = mixed[:, :, 0]
    keys = mixed[:, :, 1]
    values = mixed[:, :, 2].astype(jnp.bfloat16)
    query_len = jnp.sqrt(jnp.sum(query * query, axis=-1, keepdims=True) + NORM_EPS)
    key_len = jnp.sqrt(jnp.sum(keys * keys, axis=-1, keepdims=True) + NORM_EPS)
    query_unit = query / query_len
    key_unit = keys / key_len
    query_half = query_unit.astype(jnp.bfloat16)
    key_half = key_unit.astype(jnp.bfloat16)
    cosine = jnp.einsum("wihd,wjhd->whij", query_half, key_half, preferred_element_type=jnp.float32)
    scale = jnp.exp(log_gain)[:, None, None]
    scores = cosine * scale + BIAS_CAP * jax.nn.sigmoid(table)
    expo = jnp.where(allowed[:, None], jnp.exp(scores - scale - BIAS_CAP), 0.0)
    probs = expo / jnp.sum(expo, axis=-1, keepdims=True)
    probs_half = probs.astype(jnp.bfloat16)
    attended = jnp.einsum("whij,wjhd->wihd", probs_half, values, preferred_element_type=jnp.float32)
    attended = attended.astype(jnp.bfloat16).reshape(count * length, width)
    projected = jnp.dot(attended, w_outer, preferred_element_type=jnp.float32)
    centred = projected - jnp.mean(projected, axis=-1, keepdims=True)
    inverse = lax.rsqrt(jnp.mean(centred * centred, axis=-1, keepdims=True) + LAYER_EPS)
    normed = centred * inverse
    output = (flat.astype(jnp.float32) + normed * gain).astype(jnp.bfloat16)
    saved = (
        flat,
        query_unit,
        key_unit,
        query_len,
        key_len,
        query_half,
        key_half,
        values,
        cosine,
        probs,
        probs_half,
        attended,
        normed,
        inverse,
    )
    return (output.reshape(count, length, width), saved)


def attend_backward(upstream, saved, w_inner, w_outer, gain, log_gain, table):
    (
        flat,
        query_unit,
        key_unit,
        query_len,
        key_len,
        query_half,
        key_half,
        values,
        cosine,
        probs,
        probs_half,
        attended,
        normed,
        inverse,
    ) = saved
    count = probs.shape[0]
    heads = probs.shape[1]
    width = flat.shape[1]
    depth = width // heads
    grad_out = upstream.reshape(flat.shape[0], width).astype(jnp.float32)
    gain_term = jnp.sum(grad_out * normed, axis=0)
    scaled = grad_out * gain
    grad_proj = inverse * (
        scaled
        - jnp.mean(scaled, axis=-1, keepdims=True)
        - normed * jnp.mean(scaled * normed, axis=-1, keepdims=True)
    )
    grad_proj = grad_proj.astype(jnp.bfloat16)
    grad_att = jnp.dot(grad_proj, w_outer.T, preferred_element_type=jnp.float32)
    grad_att = grad_att.astype(jnp.bfloat16).reshape(count, -1, heads, depth)
    grad_values = jnp.einsum(
        "whij,wihd->wjhd", probs_half, grad_att, preferred_element_type=jnp.float32
    )
    grad_probs = jnp.einsum("wihd,wjhd->whij", grad_att, values, preferred_element_type=jnp.float32)
    grad_scores = probs * (grad_probs - jnp.sum(probs * grad_probs, axis=-1, keepdims=True))
    scale = jnp.exp(log_gain)
    sigma = jax.nn.sigmoid(table)
    table_term = jnp.sum(grad_scores, axis=0) * (BIAS_CAP * sigma * (1.0 - sigma))
    log_term = scale * jnp.sum(grad_scores * cosine, axis=(0, 2, 3))
    grad_cos = (grad_scores * scale[:, None, None]).astype(jnp.bfloat16)
    grad_qunit = jnp.einsum(
        "whij,wjhd->wihd", grad_cos, key_half, preferred_element_type=jnp.float32
    )
    grad_kunit = jnp.einsum(
        "whij,wihd->wjhd", grad_cos, query_half, preferred_element_type=jnp.float32
    )
    grad_query = (
        grad_qunit - query_unit * jnp.sum(query_unit * grad_qunit, axis=-1, keepdims=True)
    ) / query_len
    grad_keys = (
        grad_kunit - key_unit * jnp.sum(key_unit * grad_kunit, axis=-1, keepdims=True)
    ) / key_len
    grad_mixed = jnp.stack([grad_query, grad_keys, grad_values], axis=2)
    grad_mixed = grad_mixed.astype(jnp.bfloat16).reshape(-1, 3 * width)
    grad_tokens = grad_out + jnp.dot(grad_mixed, w_inner.T, preferred_element_type=jnp.float32)
    grad_tokens = grad_tokens.astype(jnp.bfloat16).reshape(count, -1, width)
    return (grad_tokens, grad_mixed, grad_proj, (gain_term, log_term, table_term))


def reduce_weights(flat, grad_mixed, attended, grad_proj, factor):
    width = flat.shape[1]
    inner_part = jnp.einsum("tc,tk->ck", flat, grad_mixed, preferred_element_type=jnp.float32)
    outer_part = jnp.einsum("tc,tk->ck", attended, grad_proj, preferred_element_type=jnp.float32)
    summed = lax.psum_scatter(
        jnp.concatenate([inner_part, outer_part], axis=1) * factor,
        ("lon", "lat"),
        scatter_dimension=0,
        tiled=True,
    )
    return (summed[:, : 3 * width], summed[:, 3 * width :])


def local(fields, cotangent, surface, qkv_weight, proj_weight, norm_gain, log_scale, pos_table):
    margin = WIN // 2
    lon_cells, lat_cells, width = fields.shape
    lon_count = lax.axis_size("lon")
    lat_count = lax.axis_size("lat")
    lon_place = lax.axis_index("lon")
    lat_place = lax.axis_index("lat")
    factor = 1.0 / math.sqrt(lon_cells * lat_cells * lon_count * lat_count)
    corner = (lon_place * lon_cells, lat_place * lat_cells)
    own_class = lax.dynamic_slice(surface, corner, (lon_cells, lat_cells))
    rolled_class = lax.dynamic_slice(
        jnp.roll(surface, (-margin, -margin), (0, 1)), corner, (lon_cells, lat_cells)
    )
    rows_global = lat_place * lat_cells + jnp.arange(lat_cells, dtype=jnp.int32)
    north_rim = ((rows_global + margin) % (lat_cells * lat_count) < margin).astype(jnp.int32)
    rolled_key = rolled_class * 2 + north_rim[None, :]
    allow_first = pair_mask(to_windows(own_class))
    allow_second = pair_mask(to_windows(rolled_key))
    first = (qkv_weight[0], proj_weight[0], norm_gain[0], log_scale[0], pos_table[0])
    second = (qkv_weight[1], proj_weight[1], norm_gain[1], log_scale[1], pos_table[1])
    hidden, saved_first = attend_forward(to_windows(fields), allow_first, *first)
    stacked = jnp.stack([from_windows(hidden, lon_cells, lat_cells), cotangent])
    moved = roll_lat(roll_lon(stacked, -1, margin), -1, margin)
    _, saved_second = attend_forward(to_windows(moved[0]), allow_second, *second)
    grad_second, mixed_second, proj_second, small_second = attend_backward(
        to_windows(moved[1]), saved_second, *second
    )
    small_second = tuple((term * factor for term in small_second))
    weights_second = reduce_weights(
        saved_second[0], mixed_second, saved_second[11], proj_second, factor
    )
    back_tile = from_windows(grad_second, lon_cells, lat_cells)[None]
    returned = roll_lon(roll_lat(back_tile, 1, margin), 1, margin)[0]
    grad_first, mixed_first, proj_first, small_first = attend_backward(
        to_windows(returned), saved_first, *first
    )
    small_first = tuple((term * factor for term in small_first))
    weights_first = reduce_weights(saved_first[0], mixed_first, saved_first[11], proj_first, factor)
    merged = lax.psum(
        (
            jnp.stack([small_first[0], small_second[0]]),
            jnp.stack([small_first[1], small_second[1]]),
            jnp.stack([small_first[2], small_second[2]]),
        ),
        ("lon", "lat"),
    )
    d_fields = from_windows(grad_first, lon_cells, lat_cells)
    d_qkv = jnp.stack([weights_first[0], weights_second[0]])
    d_proj = jnp.stack([weights_first[1], weights_second[1]])
    return (d_fields, d_qkv, d_proj, merged[0], merged[1], merged[2])


def solution(mesh):
    placed = (P("lon", "lat", None), P("lon", "lat", None), P(), P(), P(), P(), P(), P())
    return jax.shard_map(
        local,
        mesh=mesh,
        in_specs=placed,
        out_specs=(
            P("lon", "lat", None),
            P(None, ("lon", "lat"), None),
            P(None, ("lon", "lat"), None),
            P(),
            P(),
            P(),
        ),
        check_vma=False,
    )
```

profile of v0, /device:TPU:1, one launch (start us, length us, event | category | flops | bytes accessed | tf_op | source)
XLA Modules:
  0.0 326.7 jit_solution(3618756749405340268)
XLA Ops:
  10.8 2.2 fusion.157
  13.3 3.8 %slice_bitcast_fusion = (bf16[1536,512]{0,1:T(8,128)(2,1)}, bf16[1536,512]{0,1:T(8,128)(2,1)}) fusion(bf16[2,512,1536]{2,1,0:T(8,128)(2,1)} %param.11), kind=kLoop, calls=%fused_computation.27 | loop fusion | bytes 6291456 | tf_op jit(solution)/shard_map/dot_general | solution.py:63
  17.1 1.8 copy.112
  24.9 1.6 fusion.159
  27.7 7.1 %collective-permute-start = (bf16[2,4,32,512]{3,2,1,0:T(8,128)(2,1)}, bf16[2,4,32,512]{3,2,1,0:T(8,128)(2,1)}, u32[]{:S(2)}, u32[]{:S(2)}) collective-permute-start(bf16[2,4,32,512]{3,2,1,0:T(8,128)(2,1)} %get-tuple-element.54), channel_id=1, source_target_pairs={{4,0},{8,4},{12,8},{16,12},{20,16},{24,20},{28,24},{32,28},{36,32}... | collective-permute-start | bytes 786440 | tf_op jit(solution)/shard_map/ppermute | solution.py:19
  35.3 2.0 copy.170
  37.4 2.6 copy.121
  40.0 2.0 multiply_bitcast_fusion
  42.8 1.2 collective-permute-start.1
  44.0 1.1 slice_maximum_fusion
  45.1 4.0 %collective-permute-done.1 = bf16[2,8,4,512]{3,2,1,0:T(4,128)(2,1)S(1)} collective-permute-done((bf16[2,8,4,512]{3,2,1,0:T(4,128)(2,1)S(1)}, bf16[2,8,4,512]{3,2,1,0:T(4,128)(2,1)S(1)}, u32[]{:S(2)}, u32[]{:S(2)}) %collective-permute-start.1) | collective-permute-done | bytes 65568 | tf_op jit(solution)/shard_map/ppermute | solution.py:19
  49.4 1.2 fusion.99
  57.0 1.3 copy-done
  58.7 1.2 copy.126
  59.9 1.5 reshape.240
  61.4 1.6 fusion.160
  65.3 1.3 fusion.162
  68.8 3.4 %fusion.44 = bf16[4,64,1,16,32]{1,4,3,0,2:T(8,128)(2,1)} fusion(f32[4,16,64,64]{2,3,1,0:T(8,128)} %copy-done, bf16[4,64,16,32]{1,0,3,2:T(4,128)(2,1)} %reshape.241), kind=kOutput, calls=%fused_computation.65 | convolution fusion | flops 17170432 | bytes 1572864 | tf_op jit(solution)/shard_map/whij,wihd->wjhd/dot_general | solution.py:138
  72.1 1.9 fusion.88
  74.0 1.4 copy-done.8
  75.4 1.7 fusion.156
  77.1 5.7 %convolution_bitcast_fusion.3 = f32[4,64,16,32]{1,3,2,0:T(8,128)} fusion(f32[16]{0:T(128)S(1)} %get-tuple-element.59, f32[4,16,64,64]{2,3,1,0:T(8,128)} %copy-done, f32[4,16,64,64]{2,3,1,0:T(8,128)} %copy-done.8, f32[4,64,3,16,32]{1,4,3,2,0:T(8,128)} %copy-done.3, f32[4,64,16]{1,2,0:T(8,128)S(1)} %add_sqrt_fusion), kind=kOutput, calls=%fused_computation.45 | convolution fusion | flops 18354240 | bytes 9977920 | tf_op jit(solution)/shard_map/whij,wihd->wjhd/dot_general | solution.py:151
  82.7 5.6 %convolution_bitcast_fusion.4 = f32[4,64,16,32]{1,3,2,0:T(8,128)} fusion(f32[16]{0:T(128)S(1)} %get-tuple-element.59, f32[4,16,64,64]{2,3,1,0:T(8,128)} %copy-done, f32[4,16,64,64]{2,3,1,0:T(8,128)} %copy-done.8, f32[4,64,3,16,32]{1,4,3,2,0:T(8,128)} %copy-done.3, f32[4,64,16]{1,2,0:T(8,128)S(1)} %add_sqrt_fusion.1), kind=kOutput, calls=%fused_computation.46 | convolution fusion | flops 18354240 | bytes 9977920 | tf_op jit(solution)/shard_map/whij,wjhd->wihd/dot_general | solution.py:148
  88.3 2.6 fusion.39
  91.0 2.0 fusion.38
  93.3 2.4 copy.134
  95.7 3.6 %convert_element_type.162 = bf16[256,1536]{0,1:T(8,128)(2,1)} reshape(bf16[4,64,3,16,32]{1,0,4,3,2:T(4,128)(2,1)} %copy.134) | data formatting | bytes 1572864 | tf_op jit(solution)/shard_map/convert_element_type | solution.py:161
  99.3 2.5 fusion.52
  103.2 2.4 maximum_multiply_fusion.1
  106.8 7.5 %collective-permute-done.3 = bf16[1,4,32,512]{3,2,1,0:T(8,128)(2,1)S(1)} collective-permute-done((bf16[1,4,32,512]{3,2,1,0:T(8,128)(2,1)S(1)}, bf16[1,4,32,512]{3,2,1,0:T(8,128)(2,1)S(1)}, u32[]{:S(2)}, u32[]{:S(2)}) %collective-permute-start.3) | collective-permute-done | bytes 131104 | tf_op jit(solution)/shard_map/ppermute | solution.py:19
  116.1 1.1 fusion.72
  117.8 1.3 fusion.161
  119.5 1.5 fusion.45
  121.0 1.9 fusion.85
  122.9 1.3 copy-done.9
  125.2 4.3 %convolution_bitcast_fusion.1 = f32[4,64,16,32]{1,3,2,0:T(8,128)} fusion(f32[16]{0:T(128)S(1)} %copy-done.51, f32[4,16,64,64]{2,3,1,0:T(8,128)S(1)} %fusion.30, f32[4,16,64,64]{2,3,1,0:T(8,128)} %copy-done.9, f32[4,64,3,16,32]{1,4,3,2,0:T(8,128)} %copy-done.2, f32[4,64,16]{1,2,0:T(8,128)S(1)} %copy-done.40), kind=kOutput, calls=%fused_computation.43 | convolution fusion | flops 18354240 | bytes 7373312 | tf_op jit(solution)/shard_map/whij,wihd->wjhd/dot_general | solution.py:151
  129.4 4.2 %convolution_bitcast_fusion.2 = f32[4,64,16,32]{1,3,2,0:T(8,128)} fusion(f32[16]{0:T(128)S(1)} %copy-done.51, f32[4,16,64,64]{2,3,1,0:T(8,128)S(1)} %fusion.30, f32[4,16,64,64]{2,3,1,0:T(8,128)} %copy-done.9, f32[4,64,3,16,32]{1,4,3,2,0:T(8,128)} %copy-done.2, f32[4,64,16]{1,2,0:T(8,128)S(1)} %copy-done.42), kind=kOutput, calls=%fused_computation.44 | convolution fusion | flops 18354240 | bytes 7373312 | tf_op jit(solution)/shard_map/whij,wjhd->wihd/dot_general | solution.py:148
  134.6 2.6 fusion.41
  137.3 2.0 fusion.40
  139.7 2.4 copy.144
  142.1 2.9 convert_element_type.172
  147.3 2.5 maximum_multiply_fusion
  150.8 2.0 fusion.55
  153.6 64.0 %all-reduce.2 = (f32[2,512]{1,0:T(2,128)}, f32[2,16]{1,0:T(2,128)}) all-reduce(f32[2,512]{1,0:T(2,128)S(1)} %pad_maximum_fusion.9, f32[2,16]{1,0:T(2,128)S(1)} %pad_maximum_fusion.10), channel_id=1, replica_groups=mesh['lon'=32,'lat'=4] {'lon','lat'}, use_global_device_ids=true, to_apply=%region_24.25 | all-reduce | flops 1056 | bytes 8448 | tf_op jit(solution)/shard_map/psum | solution.py:218
  217.6 93.8 %all-reduce.6.cloned.1.call-done = (f32[512,2048]{0,1:T(8,128)}, f32[512,2048]{0,1:T(8,128)}, f32[2,16,64,64]{2,3,1,0:T(8,128)}) async-done(((f32[512,2048]{0,1:T(8,128)}, f32[512,2048]{0,1:T(8,128)}, f32[2,16,64,64]{2,3,1,0:T(8,128)}), (f32[512,2048]{0,1:T(8,128)}, f32[512,2048]{0,1:T(8,128)}, f32[2,16,64,64]{2,3,1,0:T(8,128)})) %all-reduce.6.cloned.1.call-update) | async-done | bytes 8912912
  311.5 1.5 dynamic-slice_bitcast_fusion
  315.1 1.4 dynamic-slice_bitcast_fusion.1
  316.5 1.3 copy.151
  (206 shorter events, 40.0 us)
Async XLA Ops:
  7.2 304.3 %all-reduce.6.cloned.1.call-start = ((), (), s32[]{:S(2)}) async-start(), calls=%async_computation | async-start | bytes 18874368
  8.0 13.6 %copy-start.50 = (f32[16]{0:T(128)}, f32[16]{0:T(128)S(1)}, u32[]{:S(2)}) copy-start(f32[16]{0:T(128)S(1)} %get-tuple-element.60) | copy-start | bytes 196
  8.8 105.6 %copy-start.37 = (f32[1,512]{1,0:T(1,128)}, f32[1,512]{1,0:T(1,128)S(1)}, u32[]{:S(2)}) copy-start(f32[1,512]{1,0:T(1,128)S(1)} %get-tuple-element.56) | copy-start | bytes 6148
  10.8 15.9 %copy-start.20 = (bf16[1,8,4,8,512]{4,3,1,2,0:T(8,128)(2,1)}, bf16[1,8,4,8,512]{4,3,1,2,0:T(8,128)(2,1)S(1)}, u32[]{:S(2)}) copy-start(bf16[1,8,4,8,512]{4,3,1,2,0:T(8,128)(2,1)S(1)} %copy.111) | copy-start | bytes 786436
  17.1 1.8 copy-start.29
  19.9 2.4 copy-start.2
  21.6 1.4 copy-start.4
  24.9 2.0 copy-start.35
  24.9 9.9 %copy-start.36 = (s32[256,128]{1,0:T(8,128)S(1)}, s32[256,128]{1,0:T(8,128)}, u32[]{:S(2)}) copy-start(s32[256,128]{1,0:T(8,128)} %param.10) | copy-start | bytes 393220
  26.4 8.5 %copy-start.43 = (f32[256]{0:T(256)}, f32[256]{0:T(256)S(1)}, u32[]{:S(2)}) copy-start(f32[256]{0:T(256)S(1)} %broadcast_multiply_fusion.5) | copy-start | bytes 3076
  26.7 8.1 %copy-start.45 = (f32[256]{0:T(256)}, f32[256]{0:T(256)S(1)}, u32[]{:S(2)}) copy-start(f32[256]{0:T(256)S(1)} %add_rsqrt_fusion.1) | copy-start | bytes 3076
  27.7 14.3 %collective-permute-start = (bf16[2,4,32,512]{3,2,1,0:T(8,128)(2,1)}, bf16[2,4,32,512]{3,2,1,0:T(8,128)(2,1)}, u32[]{:S(2)}, u32[]{:S(2)}) collective-permute-start(bf16[2,4,32,512]{3,2,1,0:T(8,128)(2,1)} %get-tuple-element.54), channel_id=1, source_target_pairs={{4,0},{8,4},{12,8},{16,12},{20,16},{24,20},{28,24},{32,28},{36,32}... | collective-permute-start | bytes 786440 | tf_op jit(solution)/shard_map/ppermute | solution.py:19
  42.8 6.3 %collective-permute-start.1 = (bf16[2,8,4,512]{3,2,1,0:T(4,128)(2,1)S(1)}, bf16[2,8,4,512]{3,2,1,0:T(4,128)(2,1)S(1)}, u32[]{:S(2)}, u32[]{:S(2)}) collective-permute-start(bf16[2,8,4,512]{3,2,1,0:T(4,128)(2,1)S(1)} %pad_maximum_fusion.6), channel_id=1, source_target_pairs={{1,0},{2,1},{3,2},{0,3},{5,4},{6,5},{7,6},{4,7},{9,8},{10,9},{11,1... | collective-permute-start | bytes 196616 | tf_op jit(solution)/shard_map/ppermute | solution.py:19
  45.1 4.1 %copy-start.15 = (bf16[2,8,28,512]{3,2,1,0:T(8,128)(2,1)}, bf16[2,8,28,512]{3,2,1,0:T(8,128)(2,1)S(1)}, u32[]{:S(2)}) copy-start(bf16[2,8,28,512]{3,2,1,0:T(8,128)(2,1)S(1)} %slice_maximum_fusion) | copy-start | bytes 1376260
  49.4 2.8 copy-start.10
  53.2 3.2 copy-start.3
  53.3 1.4 copy-start.23
  61.4 1.8 copy-start.14
  61.4 2.8 copy-start.31
  68.8 3.4 %copy-start.16 = (bf16[4,64,16,32]{1,0,3,2:T(4,128)(2,1)S(1)}, bf16[4,64,16,32]{1,0,3,2:T(4,128)(2,1)}, u32[]{:S(2)}) copy-start(bf16[4,64,16,32]{1,0,3,2:T(4,128)(2,1)} %reshape.241) | copy-start | bytes 786436
  68.8 6.6 %copy-start.7 = (f32[4,16,64,64]{2,3,1,0:T(8,128)S(1)}, f32[4,16,64,64]{2,3,1,0:T(8,128)}, u32[]{:S(2)}) copy-start(f32[4,16,64,64]{2,3,1,0:T(8,128)} %copy-done.6) | copy-start | bytes 3145732
  72.1 3.3 %copy-start.1 = (f32[4,16,64,64]{2,3,1,0:T(8,128)S(1)}, f32[4,16,64,64]{2,3,1,0:T(8,128)}, u32[]{:S(2)}) copy-start(f32[4,16,64,64]{2,3,1,0:T(8,128)} %copy-done) | copy-start | bytes 3145732
  74.0 1.4 copy-start.8
  88.3 2.6 copy-start.54
  91.0 2.0 copy-start.28
  99.3 2.6 copy-start.19
  99.3 2.6 copy-start.30
  101.8 3.8 %collective-permute-start.2 = (bf16[1,8,4,512]{3,2,1,0:T(4,128)(2,1)S(1)}, bf16[1,8,4,512]{3,2,1,0:T(4,128)(2,1)S(1)}, u32[]{:S(2)}, u32[]{:S(2)}) collective-permute-start(bf16[1,8,4,512]{3,2,1,0:T(4,128)(2,1)S(1)} %slice.156), channel_id=1, source_target_pairs={{3,0},{0,1},{1,2},{2,3},{7,4},{4,5},{5,6},{6,7},{11,8},{8,9},{9,10... | collective-permute-start | bytes 98312 | tf_op jit(solution)/shard_map/ppermute | solution.py:19
  103.2 2.6 copy-start.11
  103.2 2.6 copy-start.26
  105.6 8.7 %copy-start.34 = (bf16[1,8,4,512]{3,2,1,0:T(4,128)(2,1)}, bf16[1,8,4,512]{3,2,1,0:T(4,128)(2,1)S(1)}, u32[]{:S(2)}) copy-start(bf16[1,8,4,512]{3,2,1,0:T(4,128)(2,1)S(1)} %collective-permute-done.2) | copy-start | bytes 98308
  105.7 8.6 %collective-permute-start.3 = (bf16[1,4,32,512]{3,2,1,0:T(8,128)(2,1)S(1)}, bf16[1,4,32,512]{3,2,1,0:T(8,128)(2,1)S(1)}, u32[]{:S(2)}, u32[]{:S(2)}) collective-permute-start(bf16[1,4,32,512]{3,2,1,0:T(8,128)(2,1)S(1)} %fusion.118), channel_id=1, source_target_pairs={{124,0},{0,4},{4,8},{8,12},{12,16},{16,20},{20,24},{24,28},{28,32}... | collective-permute-start | bytes 393224 | tf_op jit(solution)/shard_map/ppermute | solution.py:19
  115.1 2.1 copy-start.38
  115.1 2.1 copy-start.44
  115.1 2.1 copy-start.46
  115.1 2.1 copy-start.48
  115.2 2.3 copy-start.32
  116.0 1.8 copy-start.22
  121.0 3.2 copy-start.5
  125.2 4.3 %copy-start.42 = (f32[4,64,16]{1,2,0:T(8,128)S(1)}, f32[4,64,16]{1,2,0:T(8,128)}, u32[]{:S(2)}) copy-start(f32[4,64,16]{1,2,0:T(8,128)} %copy-done.41) | copy-start | bytes 49156
  134.6 2.6 copy-start.53
  137.3 2.0 copy-start.27
  139.7 5.3 %copy-start.24 = (f32[1,16,64,64]{2,3,1,0:T(8,128)S(1)}, f32[1,16,64,64]{2,3,1,0:T(8,128)}, u32[]{:S(2)}) copy-start(f32[1,16,64,64]{2,3,1,0:T(8,128)} %fusion.70) | copy-start | bytes 786436
  139.7 5.3 %copy-start.25 = (f32[1,16,64,64]{2,3,1,0:T(8,128)S(1)}, f32[1,16,64,64]{2,3,1,0:T(8,128)}, u32[]{:S(2)}) copy-start(f32[1,16,64,64]{2,3,1,0:T(8,128)} %fusion.71) | copy-start | bytes 786436
  142.1 4.0 %copy-start.21 = (bf16[1,8,4,8,512]{4,3,1,2,0:T(8,128)(2,1)S(1)}, bf16[1,8,4,8,512]{4,3,1,2,0:T(8,128)(2,1)}, u32[]{:S(2)}) copy-start(bf16[1,8,4,8,512]{4,3,1,2,0:T(8,128)(2,1)} %copy-done.20) | copy-start | bytes 786436
  149.8 3.8 %copy-start.49 = (f32[2,16]{1,0:T(2,128)S(1)}, f32[2,16]{1,0:T(2,128)}, u32[]{:S(2)}) copy-start(f32[2,16]{1,0:T(2,128)} %param.14) | copy-start | bytes 388
  149.8 3.8 %copy-start.52 = (f32[16]{0:T(128)S(1)}, f32[16]{0:T(128)}, u32[]{:S(2)}) copy-start(f32[16]{0:T(128)} %get-tuple-element.37) | copy-start | bytes 196
  311.5 5.1 %copy-start.33 = (f32[2,16,64,64]{2,3,1,0:T(8,128)S(1)}, f32[2,16,64,64]{2,3,1,0:T(8,128)}, u32[]{:S(2)}) copy-start(f32[2,16,64,64]{2,3,1,0:T(8,128)} %get-tuple-element.46) | copy-start | bytes 1572868
  (12 other events, 13.8 us)
Sparse Core Ops, SparseCore 0:
  149.9 161.5 all-reduce.5
where the time goes:
time: 328 us; the launch traced here: 327 us
  waiting for transfers between devices  105 us (32%)
  blocking collectives  64 us (20%)
  local copies, waits for them, and re-layouts  53.1 us (16%)
  matrix products  45.9 us (14%)
  other arithmetic  34.8 us (11%)
  between operations  15 us (5%)
  starting transfers between devices  8.5 us (3%)
    unnamed x2, waiting for transfers between devices  93.8 us
    psum x1, blocking collectives, local(): lax.psum((jnp.stack([small_first[0], small_second[0]]), jnp.stack([small_...  64 us
    unnamed x113, local copies, waits for them, and re-layouts  12.4 us
    ppermute x4, waiting for transfers between devices, passed_along(): return lax.ppermute(block, axis, route)  11.6 us
    dot_general x2, matrix products, attend_backward(): jnp.einsum('whij,wihd->wjhd', grad_cos, query_half, preferred_element_typ...  9.94 us
    dot_general x2, matrix products, attend_backward(): jnp.einsum('whij,wjhd->wihd', grad_cos, key_half, preferred_element_type=...  9.74 us
    ppermute x4, starting transfers between devices, passed_along(): return lax.ppermute(block, axis, route)  8.46 us
    dot_general x3, local copies, waits for them, and re-layouts, attend_forward(): mixed = jnp.dot(flat, w_inner, preferred_element_type=jnp.float32)  8.11 us
  transfers between devices with their start and end apart: 5, of which 3 were waited for; matrix products, arithmetic and copies ran while one was open for 5% of the time, Pallas kernels for 0%

commit v1 on v0

v1 whole, which is shorter than its diff:
```python
import math

import jax
import jax.numpy as jnp
import numpy as np
from jax import lax
from jax.experimental import pallas as pl
from jax.experimental.pallas import tpu as pltpu
from jax.sharding import PartitionSpec as P

WIN = 8
HALF = WIN // 2
LON, LAT = 8, 32
TOKENS = LON * LAT
WINDOWS = 4
WIDTH = 512
GROUPS = 4
PART = 768
NORM_EPS = 1e-06
LAYER_EPS = 1e-05
CAP = 16.0
F32, BF16 = jnp.float32, jnp.bfloat16
MESH = pl.DeviceIdType.MESH

ORDERS = (("x", "y", "z"), ("y", "z", "x"), ("z", "x", "y"))


def token_orders():
    cells = [(i, l) for i in range(LON) for l in range(LAT)]
    natural = {c: k for k, c in enumerate(cells)}
    windows = [(i, w * WIN + j) for w in range(WINDOWS) for i in range(WIN) for j in range(WIN)]
    spot = {c: k for k, c in enumerate(windows)}
    parts = []
    for north in (False, True):
        for west in (False, True):
            parts += [c for c in cells if (c[0] < HALF) == west and (c[1] < HALF) == north]
    to_window = np.zeros((TOKENS, TOKENS), np.float32)
    to_part = np.zeros_like(to_window)
    window_to_part = np.zeros_like(to_window)
    to_shifted = np.zeros_like(to_window)
    for k, c in enumerate(windows):
        to_window[k, natural[c]] = 1
    for k, c in enumerate(parts):
        to_part[k, natural[c]] = 1
        window_to_part[k, spot[c]] = 1
        to_shifted[spot[((c[0] - HALF) % LON, (c[1] - HALF) % LAT)], k] = 1
    picks = [to_window, window_to_part, to_part, to_shifted]
    picks += [to_window.T, window_to_part.T, to_shifted.T]
    return np.stack(picks)


def row_orders():
    orders = np.zeros((3, WIDTH, WIDTH), np.float32)
    for g, axes in enumerate(ORDERS):
        for place in range(WIDTH):
            at = dict(core=place // 256)
            for axis, step in zip(axes, (64, 16, 4)):
                at[axis] = place // step % 4
            lon = at["z"] % 2 * 16 + at["y"] * 4 + at["x"]
            lat = at["z"] // 2 * 2 + at["core"]
            orders[g, place, (lon * 4 + lat) * 4 + place % 4] = 1
    return orders


def mm(a, b):
    return jnp.dot(a, b, preferred_element_type=F32)


def mm_nt(a, b):
    return lax.dot_general(a, b, (((1,), (1,)), ((), ())), preferred_element_type=F32)


def mm_tn(a, b):
    return lax.dot_general(a, b, (((0,), (0,)), ((), ())), preferred_element_type=F32)


def iota(shape, dim):
    return lax.broadcasted_iota(jnp.int32, shape, dim)


def same_run(size, run):
    return (iota((size, size), 0) // run == iota((size, size), 1) // run).astype(F32).astype(BF16)


def run_sum(x, ones):
    high = x.astype(BF16)
    low = (x - high.astype(F32)).astype(BF16)
    return mm(high, ones) + mm(low, ones)


def scratch_spec():
    v = pltpu.VMEM
    return dict(
        x=v((2, TOKENS, WIDTH), BF16),
        grad=v((TOKENS, WIDTH), BF16),
        qunit=v((2, TOKENS, WIDTH), F32),
        kunit=v((2, TOKENS, WIDTH), F32),
        qinv=v((2, TOKENS, WIDTH), F32),
        kinv=v((2, TOKENS, WIDTH), F32),
        qhalf=v((2, TOKENS, WIDTH), BF16),
        khalf=v((2, TOKENS, WIDTH), BF16),
        vhalf=v((2, TOKENS, WIDTH), BF16),
        cosine=v((2, GROUPS, TOKENS, 256), F32),
        probs=v((2, GROUPS, TOKENS, 256), F32),
        attended=v((2, TOKENS, WIDTH), BF16),
        normed=v((2, TOKENS, WIDTH), F32),
        inverse=v((2, TOKENS, 1), F32),
        dz=v((TOKENS, WIDTH), BF16),
        datt=v((TOKENS, WIDTH), BF16),
        dmixed=v((TOKENS, 3 * WIDTH), BF16),
        bias=v((2, GROUPS, 64, 256), F32),
        slope=v((2, GROUPS, 64, 256), F32),
        scale=v((2, GROUPS, 1, 256), F32),
        mask=v((2, TOKENS, 256), F32),
        dtab=v((GROUPS, 64, 256), F32),
        dlog=v((GROUPS, 1, 256), F32),
        hid_out=v((TOKENS, WIDTH), BF16),
        hid_in=v((TOKENS, WIDTH), BF16),
        cot_out=v((TOKENS, WIDTH), BF16),
        cot_in=v((TOKENS, WIDTH), BF16),
        back_out=v((TOKENS, WIDTH), BF16),
        back_in=v((TOKENS, WIDTH), BF16),
        part=v((2, 3, WIDTH, PART), BF16),
        r1=v((2, 3, 256, PART), BF16),
        s1=v((2, 3, 256, PART), BF16),
        r2=v((2, 3, 3, 64, PART), BF16),
        s2=v((2, 3, 64, PART), BF16),
        r3=v((2, 3, 3, 16, PART), BF16),
        r4=v((2, 3, 4, 16, PART), BF16),
        small=v((2, WIDTH, 256), BF16),
        send=pltpu.SemaphoreType.DMA((96,)),
        recv=pltpu.SemaphoreType.DMA((96,)),
    )


class Refs:
    pass


class Links:
    def __init__(self, r):
        self.r = r
        self.count = 0
        self.started = []
        lon, lat = lax.axis_index("lon"), lax.axis_index("lat")
        self.lon, self.lat = lon, lat
        self.core = lat % 2
        self.at = dict(x=lon % 4, y=lon // 4 % 4, z=lat // 2 * 2 + lon // 16)

    def along(self, axis, to):
        at = dict(self.at)
        at[axis] = to
        return (at["z"] % 2 * 16 + at["y"] * 4 + at["x"], at["z"] // 2 * 2 + self.core)

    def sibling(self):
        return (self.lon, self.lat // 2 * 2 + 1 - self.core)

    def shifted(self, dlon, dlat):
        return ((self.lon + dlon + 32) % 32, (self.lat + dlat + 4) % 4)

    def meet(self):
        barrier = pltpu.get_barrier_semaphore()
        others = [self.sibling()]
        for axis in ("x", "y", "z"):
            others += [self.along(axis, (self.at[axis] + d) % 4) for d in (1, 2, 3)]
        for d in (-1, 1):
            others += [self.shifted(d, 0), self.shifted(0, d), self.shifted(d, d)]
        for other in others:
            pl.semaphore_signal(barrier, inc=1, device_id=other, device_id_type=MESH)
        pl.semaphore_wait(barrier, len(others))

    def send(self, src, dst, to):
        k = self.count
        self.count += 1
        copy = pltpu.make_async_remote_copy(
            src_ref=src, dst_ref=dst, send_sem=self.r.send.at[k], recv_sem=self.r.recv.at[k],
            device_id=to, device_id_type=MESH,
        )
        copy.start()
        self.started.append(copy)
        return copy

    def finish(self):
        for copy in self.started:
            copy.wait_send()

    def halo(self, src, dst, sign):
        dst[0:112, :] = src[0:112, :]
        spans = ((112, 112, (sign, 0)), (224, 16, (0, sign)), (240, 16, (sign, sign)))
        return [
            self.send(src.at[pl.ds(o, n)], dst.at[pl.ds(o, n)], self.shifted(*to))
            for o, n, to in spans
        ]


class Reduce:
    def __init__(self, r, links, b, g):
        self.r, self.links, self.b, self.g = r, links, b, g
        self.axes = ORDERS[g]
        self.place = [links.at[a] for a in self.axes]
        self.step = 0

    def peers(self, level):
        axis, place = self.axes[level], self.place[level]
        return [((place + d) % 4, d) for d in (1, 2, 3)]

    def rows(self, at, size):
        return pl.ds(pl.multiple_of(at * size, size), size)

    def advance(self):
        r, links, b, g = self.r, self.links, self.b, self.g
        step = self.step
        self.step += 1
        if step == 0:
            src = r.part.at[b, g, self.rows(1 - links.core, 256)]
            self.waits = [links.send(src, r.r1.at[b, g], links.sibling())]
            return
        for copy in self.waits:
            copy.wait_recv()
        if step == 1:
            own = r.part[b, g, self.rows(links.core, 256), :].astype(F32)
            r.s1[b, g] = (own + r.r1[b, g].astype(F32)).astype(BF16)
            self.waits = [
                links.send(r.s1.at[b, g, self.rows(k, 64)], r.r2.at[b, g, d - 1], links.along(self.axes[0], k))
                for k, d in self.peers(0)
            ]
        elif step == 2:
            total = r.s1[b, g, self.rows(self.place[0], 64), :].astype(F32)
            for d in range(3):
                total += r.r2[b, g, d].astype(F32)
            r.s2[b, g] = total.astype(BF16)
            self.waits = [
                links.send(r.s2.at[b, g, self.rows(k, 16)], r.r3.at[b, g, d - 1], links.along(self.axes[1], k))
                for k, d in self.peers(1)
            ]
        elif step == 3:
            total = r.s2[b, g, self.rows(self.place[1], 16), :].astype(F32)
            for d in range(3):
                total += r.r3[b, g, d].astype(F32)
            mine = r.r4.at[b, g, self.place[2]]
            mine[...] = total.astype(BF16)
            self.waits = [links.send(mine, mine, links.along(self.axes[2], k)) for k, d in self.peers(2)]
        elif step == 4:
            total = r.r4[b, g, 0].astype(F32)
            for k in range(1, 4):
                total += r.r4[b, g, k].astype(F32)
            own = total[0:4, :]
            for k in range(1, 4):
                own = jnp.where(self.place[2] == k, total[4 * k : 4 * k + 4, :], own)
            if g == 0:
                r.d_proj[b] = own[:, 0:WIDTH]
                at = links.core * 16 + self.place[0] * 4 + self.place[1]
                mine = r.small.at[b, self.rows(at, 16)]
                mine[...] = total[:, WIDTH:PART].astype(BF16)
                self.waits = [links.send(mine, mine, links.along(self.axes[1], k)) for k, d in self.peers(1)]
            else:
                r.d_qkv[b, :, (g - 1) * PART : g * PART] = own
        elif step == 5:
            mine = r.small.at[b, self.rows(links.core * 4 + self.place[0], 64)]
            self.waits = [links.send(mine, mine, links.along(self.axes[0], k)) for k, d in self.peers(0)]
        elif step == 6:
            mine = r.small.at[b, self.rows(links.core, 256)]
            self.waits = [links.send(mine, mine, links.sibling())]
        elif step == 7:
            for h in range(16):
                piece = r.small[b, (h // 2) * 64 : (h // 2) * 64 + 64, 0:128].astype(F32)
                r.d_table[b, h] = piece[:, h % 2 * 64 : h % 2 * 64 + 64]
            rest = r.small[b, 0:16, 128:256].astype(F32)
            for k in range(4):
                r.d_gain[b : b + 1, k * 128 : k * 128 + 128] = rest[k : k + 1, :]
            lane = iota((1, 16), 1)
            row = jnp.zeros((1, 16), F32)
            for h in range(16):
                spot = rest[8 + h // 2 : 9 + h // 2, h % 2 * 64 : h % 2 * 64 + 1]
                row = jnp.where(lane == h, spot, row)
            r.d_log[b : b + 1, :] = row


def tables(r, b):
    lane = iota((1, 256), 1) // 64
    for g in range(GROUPS):
        logs = jnp.full((1, 256), 0.0, F32) + r.log_scale[b, 4 * g]
        for h in range(1, 4):
            logs = jnp.where(lane == h, r.log_scale[b, 4 * g + h], logs)
        scale = jnp.exp(logs)
        sigma = jnp.concatenate([r.pos_table[b, 4 * g + h] for h in range(4)], axis=1)
        sigma = 1.0 / (1.0 + jnp.exp(-sigma))
        r.scale[b, g] = scale
        r.bias[b, g] = CAP * sigma - scale - CAP
        r.slope[b, g] = CAP * sigma * (1.0 - sigma)


def masks(r, links, b):
    shift = HALF * b
    first = r.surface[pl.ds(pl.multiple_of(links.lon * LON, LON), LON), :]
    later = r.surface[pl.ds(pl.multiple_of((links.lon + 1) % 32 * LON, LON), LON), :]
    slab = jnp.concatenate([first, later], axis=0).astype(F32).astype(BF16)

    def column(w, t):
        return (links.lat * LAT + w * WIN + t % WIN + shift) % 128

    def labels(found, col):
        return found * 2.0 + (col < shift).astype(F32)

    for w in range(WINDOWS):
        tok = iota((128, 256), 1) % 64
        pick = (iota((128, 256), 0) == column(w, tok)).astype(F32).astype(BF16)
        wide = mm(slab, pick)
        tok = iota((16, 256), 1) % 64
        found = jnp.sum(jnp.where(iota((16, 256), 0) == tok // WIN + shift, wide, 0.0), axis=0, keepdims=True)
        along = labels(found, column(w, iota((1, 256), 1) % 64))
        tok = iota((64, 128), 0)
        pick = (iota((64, 128), 1) == column(w, tok)).astype(F32).astype(BF16)
        tall = mm_nt(pick, slab)
        tok = iota((64, 16), 0)
        found = jnp.sum(jnp.where(iota((64, 16), 1) == tok // WIN + shift, tall, 0.0), axis=1, keepdims=True)
        down = labels(found, column(w, iota((64, 1), 0)))
        r.mask[b, w * 64 : w * 64 + 64, :] = (down == along).astype(F32)


def group_lanes(g, base=0):
    return pl.ds(pl.multiple_of(base + g * 128, 128), 128)


def head_lanes(dtype):
    lane = iota((1, 128), 1) // 32
    return [(lane == h).astype(F32).astype(dtype) for h in range(4)]


def expand(block, lanes):
    return jnp.concatenate([block * lanes[h] for h in range(4)], axis=0)


def collapse(block, lanes):
    return sum(block[h * 64 : h * 64 + 64, :] * lanes[h] for h in range(4))


def window(x, w):
    return x[w * 64 : w * 64 + 64, :]


def forward(r, b, last):
    x = r.x[b]
    ones32 = same_run(256, 32)
    for name, k in (("q", 0), ("k", 1)):
        mixed = mm(x, r.qkv_weight[b, :, k * WIDTH : (k + 1) * WIDTH])
        square = mixed * mixed
        total = jnp.concatenate([run_sum(square[:, o : o + 256], ones32) for o in (0, 256)], axis=1)
        inv = lax.rsqrt(total + NORM_EPS)
        unit = mixed * inv
        getattr(r, name + "inv")[b] = inv
        getattr(r, name + "unit")[b] = unit
        getattr(r, name + "half")[b] = unit.astype(BF16)
    r.vhalf[b] = mm(x, r.qkv_weight[b, :, 2 * WIDTH : 3 * WIDTH]).astype(BF16)

    def attend(g, carry):
        cols = group_lanes(g)
        lanes = head_lanes(BF16)
        ones64 = same_run(256, 64)
        q, k, v = r.qhalf[b, :, cols], r.khalf[b, :, cols], r.vhalf[b, :, cols]
        cosine = jnp.concatenate(
            [mm_nt(window(q, w), expand(window(k, w), lanes)) for w in range(WINDOWS)], axis=0
        )
        r.cosine[b, g] = cosine
        bias = jnp.concatenate([r.bias[b, g]] * WINDOWS, axis=0)
        expo = jnp.exp(cosine * r.scale[b, g] + bias) * r.mask[b]
        probs = expo / run_sum(expo, ones64)
        r.probs[b, g] = probs
        half = probs.astype(BF16)
        out = [mm(window(half, w), expand(window(v, w), lanes)) for w in range(WINDOWS)]
        r.attended[b, :, cols] = jnp.concatenate(out, axis=0).astype(BF16)
        return carry

    lax.fori_loop(0, GROUPS, attend, 0)
    z = mm(r.attended[b], r.proj_weight[b])
    centred = z - jnp.mean(z, axis=-1, keepdims=True)
    inverse = lax.rsqrt(jnp.mean(centred * centred, axis=-1, keepdims=True) + LAYER_EPS)
    normed = centred * inverse
    r.inverse[b] = inverse
    r.normed[b] = normed
    if last:
        return None
    return (x.astype(F32) + normed * r.norm_gain[b : b + 1, :]).astype(BF16)


def backward_norm(r, b, factor):
    grad = r.grad[...].astype(F32)
    normed = r.normed[b]
    gain_term = jnp.sum(grad * normed, axis=0, keepdims=True) * factor
    for k in range(4):
        r.part[b, 0, 0:16, 640:768] = jnp.where(
            iota((16, 128), 0) == k, gain_term[:, k * 128 : k * 128 + 128], r.part[b, 0, 0:16, 640:768].astype(F32)
        ).astype(BF16)
    scaled = grad * r.norm_gain[b : b + 1, :]
    first = jnp.mean(scaled, axis=-1, keepdims=True)
    second = jnp.mean(scaled * normed, axis=-1, keepdims=True)
    dz = (r.inverse[b] * (scaled - first - normed * second)).astype(BF16)
    r.dz[...] = dz
    r.datt[...] = mm_nt(dz, r.proj_weight[b]).astype(BF16)


def backward_attend(r, b, begin, end):
    def attend(g, carry):
        cols = group_lanes(g)
        lanes, wide = head_lanes(BF16), head_lanes(F32)
        ones64, ones32 = same_run(256, 64), same_run(128, 32)
        q, k, v = r.qhalf[b, :, cols], r.khalf[b, :, cols], r.vhalf[b, :, cols]
        datt = r.datt[:, cols]
        probs = r.probs[b, g]
        half = probs.astype(BF16)
        dprobs = jnp.concatenate(
            [mm_nt(window(datt, w), expand(window(v, w), lanes)) for w in range(WINDOWS)], axis=0
        )
        dscores = probs * (dprobs - run_sum(probs * dprobs, ones64))
        r.dtab[g] = sum(window(dscores, w) for w in range(WINDOWS))
        r.dlog[g] = jnp.sum(dscores * r.cosine[b, g], axis=0, keepdims=True)
        dcos = (dscores * r.scale[b, g]).astype(BF16)
        dq, dk, dv = [], [], []
        for w in range(WINDOWS):
            dq.append(mm(window(dcos, w), expand(window(k, w), lanes)))
            dk.append(collapse(mm_tn(window(dcos, w), window(q, w)), wide))
            dv.append(collapse(mm_tn(window(half, w), window(datt, w)), wide))
        for base, parts, unit, inv in ((0, dq, r.qunit, r.qinv), (WIDTH, dk, r.kunit, r.kinv)):
            grad = jnp.concatenate(parts, axis=0)
            unit = unit[b, :, cols]
            grad = (grad - unit * run_sum(unit * grad, ones32)) * inv[b, :, cols]
            r.dmixed[:, group_lanes(g, base)] = grad.astype(BF16)
        r.dmixed[:, group_lanes(g, 2 * WIDTH)] = jnp.concatenate(dv, axis=0).astype(BF16)
        return carry

    lax.fori_loop(begin, end, attend, 0)


def backward_tokens(r, b):
    grad = r.grad[...].astype(F32) + mm_nt(r.dmixed[...], r.qkv_weight[b])
    return grad.astype(BF16)


def small_part(r, b, factor):
    ones64 = same_run(256, 64)
    sums = []
    for g in range(GROUPS):
        term = (r.dtab[g] * r.slope[b, g] * factor).astype(BF16)
        r.part[b, 0, g * 128 : g * 128 + 64, 512:640] = term[:, 0:128]
        r.part[b, 0, g * 128 + 64 : g * 128 + 128, 512:640] = term[:, 128:256]
        sums.append(run_sum(jnp.concatenate([r.dlog[g]] * 8, axis=0), ones64) * (r.scale[b, g] * factor))
    row = iota((16, 128), 0)
    rest = r.part[b, 0, 0:16, 640:768].astype(F32)
    for g in range(GROUPS):
        for k in range(2):
            rest = jnp.where(row == 8 + 2 * g + k, sums[g][0:1, k * 128 : k * 128 + 128], rest)
    r.part[b, 0, 0:16, 640:768] = rest.astype(BF16)


def weight_part(r, b, g, factor):
    if g == 0:
        turned = mm_nt(r.row_order[0], r.attended[b]).astype(BF16)
        r.part[b, 0, :, 0:WIDTH] = (mm(turned, r.dz[...]) * factor).astype(BF16)
    else:
        turned = mm_nt(r.row_order[g], r.x[b]).astype(BF16)
        grad = mm(turned, r.dmixed[:, (g - 1) * PART : g * PART])
        r.part[b, g] = (grad * factor).astype(BF16)


INPUTS = (
    "fields", "cotangent", "surface", "qkv_weight", "proj_weight", "norm_gain", "log_scale", "pos_table",
    "token_order", "row_order",
)
OUTPUTS = ("d_fields", "d_qkv", "d_proj", "d_gain", "d_log", "d_table")


def pick(order, block):
    return mm(order, block).astype(BF16)


def kernel(factor, *refs):
    r = Refs()
    for name, ref in zip(INPUTS + OUTPUTS + tuple(scratch_spec()), refs):
        setattr(r, name, ref)
    links = Links(r)
    links.meet()
    to_window, window_to_part, to_part, to_shifted, from_window, part_to_window, from_shifted = range(7)
    order = r.token_order

    r.cot_out[...] = pick(order[to_part], r.cotangent[...])
    cot = links.halo(r.cot_out, r.cot_in, -1)
    for b in range(2):
        tables(r, b)
        masks(r, links, b)
        r.part[b, 0, :, 640:768] = jnp.zeros((WIDTH, 128), BF16)
    r.x[0] = pick(order[to_window], r.fields[...])
    hidden = forward(r, 0, False)
    r.hid_out[...] = pick(order[window_to_part], hidden)
    hid = links.halo(r.hid_out, r.hid_in, -1)
    for copy in cot + hid:
        copy.wait_recv()
    r.x[1] = pick(order[to_shifted], r.hid_in[...])
    r.grad[...] = pick(order[to_shifted], r.cot_in[...])
    forward(r, 1, True)
    backward_norm(r, 1, factor)
    backward_attend(r, 1, 0, GROUPS)
    r.back_out[...] = pick(order[from_shifted], backward_tokens(r, 1))
    back = links.halo(r.back_out, r.back_in, 1)
    second = [Reduce(r, links, 1, g) for g in range(3)]
    first = [Reduce(r, links, 0, g) for g in range(3)]
    small_part(r, 1, factor)
    for g in range(3):
        weight_part(r, 1, g, factor)
        second[g].advance()
    for copy in back:
        copy.wait_recv()
    r.grad[...] = pick(order[part_to_window], r.back_in[...])
    backward_norm(r, 0, factor)
    for job in second:
        job.advance()
    for g in range(GROUPS):
        backward_attend(r, 0, g, g + 1)
        for job in second:
            if g < 3:
                job.advance()
    small_part(r, 0, factor)
    weight_part(r, 0, 0, factor)
    first[0].advance()
    second[0].advance()
    for g in (1, 2):
        weight_part(r, 0, g, factor)
        first[g].advance()
    second[0].advance()
    r.d_fields[...] = pick(order[from_window], backward_tokens(r, 0))
    second[0].advance()
    for step in range(4):
        for job in first:
            job.advance()
    for step in range(3):
        first[0].advance()
    links.finish()


def local(fields, cotangent, surface, qkv_weight, proj_weight, norm_gain, log_scale, pos_table):
    factor = 1.0 / math.sqrt(TOKENS * 128)
    shape = jax.ShapeDtypeStruct
    orders = [jnp.asarray(x, BF16) for x in (token_orders(), row_orders())]
    vmem = pl.BlockSpec(memory_space=pltpu.VMEM)
    smem = pl.BlockSpec(memory_space=pltpu.SMEM)

    def body(*refs):
        kernel(factor, *refs)

    out = pl.pallas_call(
        body,
        out_shape=[
            shape((TOKENS, WIDTH), BF16),
            shape((2, 4, 3 * WIDTH), F32),
            shape((2, 4, WIDTH), F32),
            shape((2, WIDTH), F32),
            shape((2, 16), F32),
            shape((2, 16, 64, 64), F32),
        ],
        in_specs=[vmem] * 6 + [smem] + [vmem] * 3,
        out_specs=[vmem] * 6,
        scratch_shapes=list(scratch_spec().values()),
        compiler_params=pltpu.CompilerParams(
            collective_id=0, has_side_effects=True, vmem_limit_bytes=60 * 1024 * 1024
        ),
    )(
        fields.reshape(TOKENS, WIDTH), cotangent.reshape(TOKENS, WIDTH), surface, qkv_weight, proj_weight,
        norm_gain, log_scale, pos_table, *orders,
    )
    return (out[0].reshape(LON, LAT, WIDTH),) + tuple(out[1:])


def solution(mesh):
    placed = (P("lon", "lat", None), P("lon", "lat", None), P(), P(), P(), P(), P(), P())
    return jax.shard_map(
        local,
        mesh=mesh,
        in_specs=placed,
        out_specs=(
            P("lon", "lat", None),
            P(None, ("lon", "lat"), None),
            P(None, ("lon", "lat"), None),
            P(),
            P(),
            P(),
        ),
        check_vma=False,
    )
```

time: 328 us -> 101 us (0.31)
  waiting for transfers between devices: 105 us -> 0 us
  Pallas kernels: 0 us -> 91.1 us
  blocking collectives: 64 us -> 0 us
  matrix products: 45.9 us -> 0 us
  local copies, waits for them, and re-layouts: 53.1 us -> 9.23 us
  other arithmetic: 34.8 us -> 0 us
  between operations: 15 us -> 0.65 us
  starting transfers between devices: 8.5 us -> 0 us
    unnamed x2 -> x0, waiting for transfers between devices: 93.8 us -> none
    pallas_call x0 -> x1, Pallas kernels: none -> 91.1 us  [local(): pl.pallas_call(body, out_shape=[shape((TOKENS, WIDTH), BF16), shape((2, 4...]
    psum x1 -> x0, blocking collectives: 64 us -> none  [local(): lax.psum((jnp.stack([small_first[0], small_second[0]]), jnp.stack([small_...]
    dot_general x24 -> x0, matrix products: 45.9 us -> none  [the longest x2 9.94 us: attend_backward(): jnp.einsum('whij,wihd->wjhd', grad_cos, query_half, preferred_element_typ...]
    mul x11 -> x0, other arithmetic: 16.2 us -> none  [the longest x2 5.24 us: attend_backward(): key_unit * jnp.sum(key_unit * grad_kunit, axis=-1, keepdims=True)]
    ppermute x4 -> x0, waiting for transfers between devices: 11.6 us -> none  [passed_along(): return lax.ppermute(block, axis, route)]
    another operation x12 -> x0, local copies, waits for them, and re-layouts: 11.3 us -> none  [the longest x2 4.76 us: attend_backward(): grad_mixed = jnp.stack([grad_query, grad_keys, grad_values], axis=2)]
    convert_element_type x8 -> x0, local copies, waits for them, and re-layouts: 10.2 us -> none  [the longest x2 6.48 us: attend_backward(): grad_mixed = grad_mixed.astype(jnp.bfloat16).reshape(-1, 3 * width)]
  transfers between devices with their start and end apart: 5 -> 0, of which waited for: 3 -> 0; matrix products, arithmetic and copies ran while one was open for 5% -> 0% of each run, Pallas kernels for 0% -> 0%
where the time goes in v1:
time: 101 us
  Pallas kernels  91.1 us (90%)
  local copies, waits for them, and re-layouts  9.23 us (9%)
    pallas_call x1, Pallas kernels, local(): pl.pallas_call(body, out_shape=[shape((TOKENS, WIDTH), BF16), shape((2, 4...  91.1 us
    unnamed x6, local copies, waits for them, and re-layouts  9.23 us

profile of v1, /device:TPU:1, one launch (start us, length us, event | category | flops | bytes accessed | tf_op | source)
XLA Modules:
  0.0 101.0 jit_solution(1152476778642361237)
XLA Ops:
  0.6 91.1 %shard_map.145 = (bf16[256,512]{1,0:T(8,128)(2,1)}, f32[2,4,1536]{2,1,0:T(4,128)}, f32[2,4,512]{2,1,0:T(4,128)}, f32[2,512]{1,0:T(2,128)}, f32[2,16]{1,0:T(2,128)}, /*index=5*/f32[2,16,64,64]{3,2,1,0:T(8,128)}) custom-call(bf16[256,512]{1,0:T(8,128)(2,1)} %bitcast.3, bf16[256,512]{1,0:T(8,128)(2,1)} %bitcast.4, s32[256,128]{1,0:T(8,128)} %refs_2_.1, ...), custom_call_target="tpu_custom_call" | custom-call | tf_op jit(solution)/shard_map/pallas_call | solution.py:549
  91.7 1.7 %copy.22 = bf16[8,32,512]{2,1,0:T(8,128)(2,1)} copy(bf16[8,32,512]{2,1,0:T(8,128)(2,1)} %bitcast.5) | data formatting | bytes 524288
  93.4 1.4 %copy.23 = f32[2,4,1536]{2,1,0:T(4,128)} copy(f32[2,4,1536]{2,1,0:T(4,128)} %get-tuple-element.25) | data formatting | bytes 98304
  94.8 1.3 %copy.24 = f32[2,4,512]{2,1,0:T(4,128)} copy(f32[2,4,512]{2,1,0:T(4,128)} %get-tuple-element.26) | data formatting | bytes 32768
  96.1 1.3 %copy.25 = f32[2,512]{1,0:T(2,128)} copy(f32[2,512]{1,0:T(2,128)} %get-tuple-element.27) | data formatting | bytes 8192
  97.4 1.2 %copy.26 = f32[2,16]{1,0:T(2,128)} copy(f32[2,16]{1,0:T(2,128)} %get-tuple-element.28) | data formatting | bytes 256
  98.7 2.3 %copy.27 = f32[2,16,64,64]{3,2,1,0:T(8,128)} copy(f32[2,16,64,64]{3,2,1,0:T(8,128)} %get-tuple-element.29) | data formatting | bytes 1048576

commit v2 on v1

--- a/solution.py
+++ b/solution.py
@@ -15,7 +15,9 @@
 WINDOWS = 4
 WIDTH = 512
 GROUPS = 4
-PART = 768
+PARTS = 4
+HALFROWS = 288
+PIECE = 96
 NORM_EPS = 1e-06
 LAYER_EPS = 1e-05
 CAP = 16.0
@@ -23,6 +25,7 @@
 MESH = pl.DeviceIdType.MESH
 
 ORDERS = (("x", "y", "z"), ("y", "z", "x"), ("z", "x", "y"))
+ORDER_OF = (0, 1, 2, 2)
 
 
 def token_orders():
@@ -120,16 +123,27 @@
         cot_in=v((TOKENS, WIDTH), BF16),
         back_out=v((TOKENS, WIDTH), BF16),
         back_in=v((TOKENS, WIDTH), BF16),
-        part=v((2, 3, WIDTH, PART), BF16),
-        r1=v((2, 3, 256, PART), BF16),
-        s1=v((2, 3, 256, PART), BF16),
-        r2=v((2, 3, 3, 64, PART), BF16),
-        s2=v((2, 3, 64, PART), BF16),
-        r3=v((2, 3, 3, 16, PART), BF16),
-        r4=v((2, 3, 4, 16, PART), BF16),
-        small=v((2, WIDTH, 256), BF16),
-        send=pltpu.SemaphoreType.DMA((96,)),
-        recv=pltpu.SemaphoreType.DMA((96,)),
+        turned=v((2, PARTS, WIDTH, TOKENS), BF16),
+        part=v((2, PARTS, WIDTH, WIDTH), BF16),
+        r1=v((2, PARTS, 256, WIDTH), BF16),
+        s1=v((2, PARTS, 256, WIDTH), BF16),
+        r2=v((2, PARTS, 3, 64, WIDTH), BF16),
+        s2=v((2, PARTS, 64, WIDTH), BF16),
+        r3=v((2, PARTS, 3, 16, WIDTH), BF16),
+        r4=v((2, PARTS, 4, 16, WIDTH), BF16),
+        small=v((2, 2 * HALFROWS, 128), BF16),
+        small_r1=v((2, HALFROWS, 128), BF16),
+        small_x=v((2, 3, 3, 4, PIECE, 128), BF16),
+        send=pltpu.SemaphoreType.DMA((168,)),
+        recv=pltpu.SemaphoreType.DMA((168,)),
+        load=pltpu.SemaphoreType.DMA((24,)),
+        fields_v=v((TOKENS, WIDTH), BF16),
+        cotangent_v=v((TOKENS, WIDTH), BF16),
+        qkv_weight_v=v((2, WIDTH, 3 * WIDTH), BF16),
+        proj_weight_v=v((2, WIDTH, WIDTH), BF16),
+        pos_table_v=v((2, 16, 64, 64), F32),
+        token_order_v=v((7, TOKENS, TOKENS), BF16),
+        row_order_v=v((3, WIDTH, WIDTH), BF16),
     )
 
 
@@ -167,7 +181,10 @@
             others += [self.shifted(d, 0), self.shifted(0, d), self.shifted(d, d)]
         for other in others:
             pl.semaphore_signal(barrier, inc=1, device_id=other, device_id_type=MESH)
-        pl.semaphore_wait(barrier, len(others))
+        self.others = len(others)
+
+    def met(self):
+        pl.semaphore_wait(pltpu.get_barrier_semaphore(), self.others)
 
     def send(self, src, dst, to):
         k = self.count
@@ -193,48 +210,66 @@
         ]
 
 
+class Loads:
+    def __init__(self, r):
+        self.r = r
+        self.copies = {}
+
+    def start(self, name, at=None):
+        src, dst = getattr(self.r, name), getattr(self.r, name + "_v")
+        if at is not None:
+            src, dst = src.at[at], dst.at[at]
+        copy = pltpu.make_async_copy(src, dst, self.r.load.at[len(self.copies)])
+        copy.start()
+        self.copies[name, at] = copy
+
+    def wait(self, name, at=None):
+        self.copies[name, at].wait()
+
+
+def rows(at, size):
+    return pl.ds(pl.multiple_of(at * size, size), size)
+
+
 class Reduce:
     def __init__(self, r, links, b, g):
         self.r, self.links, self.b, self.g = r, links, b, g
-        self.axes = ORDERS[g]
+        self.axes = ORDERS[ORDER_OF[g]]
         self.place = [links.at[a] for a in self.axes]
         self.step = 0
 
     def peers(self, level):
         axis, place = self.axes[level], self.place[level]
         return [((place + d) % 4, d) for d in (1, 2, 3)]
-
-    def rows(self, at, size):
-        return pl.ds(pl.multiple_of(at * size, size), size)
 
     def advance(self):
         r, links, b, g = self.r, self.links, self.b, self.g
         step = self.step
         self.step += 1
         if step == 0:
-            src = r.part.at[b, g, self.rows(1 - links.core, 256)]
+            src = r.part.at[b, g, rows(1 - links.core, 256)]
             self.waits = [links.send(src, r.r1.at[b, g], links.sibling())]
             return
         for copy in self.waits:
             copy.wait_recv()
         if step == 1:
-            own = r.part[b, g, self.rows(links.core, 256), :].astype(F32)
+            own = r.part[b, g, rows(links.core, 256), :].astype(F32)
             r.s1[b, g] = (own + r.r1[b, g].astype(F32)).astype(BF16)
             self.waits = [
-                links.send(r.s1.at[b, g, self.rows(k, 64)], r.r2.at[b, g, d - 1], links.along(self.axes[0], k))
+                links.send(r.s1.at[b, g, rows(k, 64)], r.r2.at[b, g, d - 1], links.along(self.axes[0], k))
                 for k, d in self.peers(0)
             ]
         elif step == 2:
-            total = r.s1[b, g, self.rows(self.place[0], 64), :].astype(F32)
+            total = r.s1[b, g, rows(self.place[0], 64), :].astype(F32)
             for d in range(3):
                 total += r.r2[b, g, d].astype(F32)
             r.s2[b, g] = total.astype(BF16)
             self.waits = [
-                links.send(r.s2.at[b, g, self.rows(k, 16)], r.r3.at[b, g, d - 1], links.along(self.axes[1], k))
+                links.send(r.s2.at[b, g, rows(k, 16)], r.r3.at[b, g, d - 1], links.along(self.axes[1], k))
                 for k, d in self.peers(1)
             ]
         elif step == 3:
-            total = r.s2[b, g, self.rows(self.place[1], 16), :].astype(F32)
+            total = r.s2[b, g, rows(self.place[1], 16), :].astype(F32)
             for d in range(3):
                 total += r.r3[b, g, d].astype(F32)
             mine = r.r4.at[b, g, self.place[2]]
@@ -247,33 +282,60 @@
             own = total[0:4, :]
             for k in range(1, 4):
                 own = jnp.where(self.place[2] == k, total[4 * k : 4 * k + 4, :], own)
-            if g == 0:
-                r.d_proj[b] = own[:, 0:WIDTH]
-                at = links.core * 16 + self.place[0] * 4 + self.place[1]
-                mine = r.small.at[b, self.rows(at, 16)]
-                mine[...] = total[:, WIDTH:PART].astype(BF16)
-                self.waits = [links.send(mine, mine, links.along(self.axes[1], k)) for k, d in self.peers(1)]
+            if g == 3:
+                r.d_proj[b] = own
             else:
-                r.d_qkv[b, :, (g - 1) * PART : g * PART] = own
-        elif step == 5:
-            mine = r.small.at[b, self.rows(links.core * 4 + self.place[0], 64)]
-            self.waits = [links.send(mine, mine, links.along(self.axes[0], k)) for k, d in self.peers(0)]
-        elif step == 6:
-            mine = r.small.at[b, self.rows(links.core, 256)]
+                r.d_qkv[b, :, g * WIDTH : (g + 1) * WIDTH] = own
+
+
+class SmallSum:
+    def __init__(self, r, links, b):
+        self.r, self.links, self.b = r, links, b
+        self.step = 0
+
+    def exchange(self, level, piece):
+        r, links, b = self.r, self.links, self.b
+        axis = ORDERS[piece][level]
+        place = links.at[axis]
+        mine = r.small_x.at[b, level, piece, place]
+        return [links.send(mine, mine, links.along(axis, (place + d) % 4)) for d in (1, 2, 3)]
+
+    def advance(self):
+        r, links, b = self.r, self.links, self.b
+        step = self.step
+        self.step += 1
+        half = rows(links.core, HALFROWS)
+        if step == 0:
+            src = r.small.at[b, rows(1 - links.core, HALFROWS)]
+            self.waits = [links.send(src, r.small_r1.at[b], links.sibling())]
+            return
+        for copy in self.waits:
+            copy.wait_recv()
+        if step == 5:
+            return
+        self.waits = []
+        for piece in range(3):
+            span = slice(piece * PIECE, (piece + 1) * PIECE)
+            if step == 1:
+                first = r.small[b, rows(links.core * 3 + piece, PIECE), :].astype(F32)
+                total = first + r.small_r1[b, span, :].astype(F32)
+            else:
+                total = r.small_x[b, step - 2, piece, 0].astype(F32)
+                for k in range(1, 4):
+                    total += r.small_x[b, step - 2, piece, k].astype(F32)
+            total = total.astype(BF16)
+            if step < 4:
+                r.small_x[b, step - 1, piece, links.at[ORDERS[piece][step - 1]]] = total
+                self.waits += self.exchange(step - 1, piece)
+            else:
+                r.total[b, rows(links.core * 3 + piece, PIECE), :] = total
+        if step == 4:
+            mine = r.total.at[b, half]
             self.waits = [links.send(mine, mine, links.sibling())]
-        elif step == 7:
-            for h in range(16):
-                piece = r.small[b, (h // 2) * 64 : (h // 2) * 64 + 64, 0:128].astype(F32)
-                r.d_table[b, h] = piece[:, h % 2 * 64 : h % 2 * 64 + 64]
-            rest = r.small[b, 0:16, 128:256].astype(F32)
-            for k in range(4):
-                r.d_gain[b : b + 1, k * 128 : k * 128 + 128] = rest[k : k + 1, :]
-            lane = iota((1, 16), 1)
-            row = jnp.zeros((1, 16), F32)
-            for h in range(16):
-                spot = rest[8 + h // 2 : 9 + h // 2, h % 2 * 64 : h % 2 * 64 + 1]
-                row = jnp.where(lane == h, spot, row)
-            r.d_log[b : b + 1, :] = row
+
+
+def table_row(k):
+    return k * 64 + (HALFROWS - 256) * (k // 4)
 
 
 def tables(r, b):
@@ -283,7 +345,7 @@
         for h in range(1, 4):
             logs = jnp.where(lane == h, r.log_scale[b, 4 * g + h], logs)
         scale = jnp.exp(logs)
-        sigma = jnp.concatenate([r.pos_table[b, 4 * g + h] for h in range(4)], axis=1)
+        sigma = jnp.concatenate([r.pos_table_v[b, 4 * g + h] for h in range(4)], axis=1)
         sigma = 1.0 / (1.0 + jnp.exp(-sigma))
         r.scale[b, g] = scale
         r.bias[b, g] = CAP * sigma - scale - CAP
@@ -339,11 +401,11 @@
     return x[w * 64 : w * 64 + 64, :]
 
 
-def forward(r, b, last):
+def project(r, b):
     x = r.x[b]
     ones32 = same_run(256, 32)
     for name, k in (("q", 0), ("k", 1)):
-        mixed = mm(x, r.qkv_weight[b, :, k * WIDTH : (k + 1) * WIDTH])
+        mixed = mm(x, r.qkv_weight_v[b, :, k * WIDTH : (k + 1) * WIDTH])
         square = mixed * mixed
         total = jnp.concatenate([run_sum(square[:, o : o + 256], ones32) for o in (0, 256)], axis=1)
         inv = lax.rsqrt(total + NORM_EPS)
@@ -351,8 +413,10 @@
         getattr(r, name + "inv")[b] = inv
         getattr(r, name + "unit")[b] = unit
         getattr(r, name + "half")[b] = unit.astype(BF16)
-    r.vhalf[b] = mm(x, r.qkv_weight[b, :, 2 * WIDTH : 3 * WIDTH]).astype(BF16)
-
+    r.vhalf[b] = mm(x, r.qkv_weight_v[b, :, 2 * WIDTH : 3 * WIDTH]).astype(BF16)
+
+
+def attention(r, b):
     def attend(g, carry):
         cols = group_lanes(g)
         lanes = head_lanes(BF16)
@@ -372,7 +436,10 @@
         return carry
 
     lax.fori_loop(0, GROUPS, attend, 0)
-    z = mm(r.attended[b], r.proj_weight[b])
+
+
+def finish_block(r, b, last):
+    z = mm(r.attended[b], r.proj_weight_v[b])
     centred = z - jnp.mean(z, axis=-1, keepdims=True)
     inverse = lax.rsqrt(jnp.mean(centred * centred, axis=-1, keepdims=True) + LAYER_EPS)
     normed = centred * inverse
@@ -380,23 +447,24 @@
     r.normed[b] = normed
     if last:
         return None
-    return (x.astype(F32) + normed * r.norm_gain[b : b + 1, :]).astype(BF16)
+    return (r.x[b].astype(F32) + normed * r.norm_gain[b : b + 1, :]).astype(BF16)
 
 
 def backward_norm(r, b, factor):
     grad = r.grad[...].astype(F32)
     normed = r.normed[b]
     gain_term = jnp.sum(grad * normed, axis=0, keepdims=True) * factor
+    row = iota((32, 128), 0)
+    rest = jnp.zeros((32, 128), F32)
     for k in range(4):
-        r.part[b, 0, 0:16, 640:768] = jnp.where(
-            iota((16, 128), 0) == k, gain_term[:, k * 128 : k * 128 + 128], r.part[b, 0, 0:16, 640:768].astype(F32)
-        ).astype(BF16)
+        rest = jnp.where(row == k, gain_term[:, k * 128 : k * 128 + 128], rest)
+    r.small[b, 256:288, :] = rest.astype(BF16)
     scaled = grad * r.norm_gain[b : b + 1, :]
     first = jnp.mean(scaled, axis=-1, keepdims=True)
     second = jnp.mean(scaled * normed, axis=-1, keepdims=True)
     dz = (r.inverse[b] * (scaled - first - normed * second)).astype(BF16)
     r.dz[...] = dz
-    r.datt[...] = mm_nt(dz, r.proj_weight[b]).astype(BF16)
+    r.datt[...] = mm_nt(dz, r.proj_weight_v[b]).astype(BF16)
 
 
 def backward_attend(r, b, begin, end):
@@ -432,41 +500,40 @@
 
 
 def backward_tokens(r, b):
-    grad = r.grad[...].astype(F32) + mm_nt(r.dmixed[...], r.qkv_weight[b])
+    grad = r.grad[...].astype(F32) + mm_nt(r.dmixed[...], r.qkv_weight_v[b])
     return grad.astype(BF16)
 
 
 def small_part(r, b, factor):
     ones64 = same_run(256, 64)
-    sums = []
+    row = iota((32, 128), 0)
+    rest = r.small[b, 256:288, :].astype(F32)
     for g in range(GROUPS):
         term = (r.dtab[g] * r.slope[b, g] * factor).astype(BF16)
-        r.part[b, 0, g * 128 : g * 128 + 64, 512:640] = term[:, 0:128]
-        r.part[b, 0, g * 128 + 64 : g * 128 + 128, 512:640] = term[:, 128:256]
-        sums.append(run_sum(jnp.concatenate([r.dlog[g]] * 8, axis=0), ones64) * (r.scale[b, g] * factor))
-    row = iota((16, 128), 0)
-    rest = r.part[b, 0, 0:16, 640:768].astype(F32)
-    for g in range(GROUPS):
+        total = run_sum(jnp.concatenate([r.dlog[g]] * 8, axis=0), ones64) * (r.scale[b, g] * factor)
         for k in range(2):
-            rest = jnp.where(row == 8 + 2 * g + k, sums[g][0:1, k * 128 : k * 128 + 128], rest)
-    r.part[b, 0, 0:16, 640:768] = rest.astype(BF16)
+            at = table_row(2 * g + k)
+            r.small[b, at : at + 64, :] = term[:, k * 128 : k * 128 + 128]
+            rest = jnp.where(row == 8 + 2 * g + k, total[0:1, k * 128 : k * 128 + 128], rest)
+    r.small[b, 256:288, :] = rest.astype(BF16)
+    r.small[b, 544:576, :] = jnp.zeros((32, 128), BF16)
+
+
+def turn(r, b, g):
+    left = r.attended if g == 3 else r.x
+    r.turned[b, g] = mm_nt(r.row_order_v[ORDER_OF[g]], left[b]).astype(BF16)
 
 
 def weight_part(r, b, g, factor):
-    if g == 0:
-        turned = mm_nt(r.row_order[0], r.attended[b]).astype(BF16)
-        r.part[b, 0, :, 0:WIDTH] = (mm(turned, r.dz[...]) * factor).astype(BF16)
-    else:
-        turned = mm_nt(r.row_order[g], r.x[b]).astype(BF16)
-        grad = mm(turned, r.dmixed[:, (g - 1) * PART : g * PART])
-        r.part[b, g] = (grad * factor).astype(BF16)
+    right = r.dz[...] if g == 3 else r.dmixed[:, g * WIDTH : (g + 1) * WIDTH]
+    r.part[b, g] = (mm(r.turned[b, g], right) * factor).astype(BF16)
 
 
 INPUTS = (
     "fields", "cotangent", "surface", "qkv_weight", "proj_weight", "norm_gain", "log_scale", "pos_table",
     "token_order", "row_order",
 )
-OUTPUTS = ("d_fields", "d_qkv", "d_proj", "d_gain", "d_log", "d_table")
+OUTPUTS = ("d_fields", "d_qkv", "d_proj", "total")
 
 
 def pick(order, block):
@@ -478,62 +545,135 @@
     for name, ref in zip(INPUTS + OUTPUTS + tuple(scratch_spec()), refs):
         setattr(r, name, ref)
     links = Links(r)
+    loads = Loads(r)
+    to_window, window_to_part, to_part, to_shifted, from_window, part_to_window, from_shifted = range(7)
+    order = r.token_order_v
+    loads.start("fields")
+    loads.start("token_order")
+    loads.start("qkv_weight", 0)
+    loads.start("pos_table", 0)
+    loads.start("cotangent")
+    loads.start("proj_weight", 0)
+    loads.start("row_order")
+    loads.start("qkv_weight", 1)
+    loads.start("pos_table", 1)
+    loads.start("proj_weight", 1)
     links.meet()
-    to_window, window_to_part, to_part, to_shifted, from_window, part_to_window, from_shifted = range(7)
-    order = r.token_order
-
-    r.cot_out[...] = pick(order[to_part], r.cotangent[...])
+    second = [Reduce(r, links, 1, g) for g in range(PARTS)]
+    first = [Reduce(r, links, 0, g) for g in range(PARTS)]
+    small_second, small_first = SmallSum(r, links, 1), SmallSum(r, links, 0)
+
+    masks(r, links, 0)
+    masks(r, links, 1)
+    loads.wait("fields")
+    loads.wait("token_order")
+    r.x[0] = pick(order[to_window], r.fields_v[...])
+    loads.wait("qkv_weight", 0)
+    project(r, 0)
+    loads.wait("pos_table", 0)
+    tables(r, 0)
+    attention(r, 0)
+    loads.wait("cotangent")
+    r.cot_out[...] = pick(order[to_part], r.cotangent_v[...])
+    loads.wait("proj_weight", 0)
+    links.met()
     cot = links.halo(r.cot_out, r.cot_in, -1)
-    for b in range(2):
-        tables(r, b)
-        masks(r, links, b)
-        r.part[b, 0, :, 640:768] = jnp.zeros((WIDTH, 128), BF16)
-    r.x[0] = pick(order[to_window], r.fields[...])
-    hidden = forward(r, 0, False)
+    hidden = finish_block(r, 0, False)
     r.hid_out[...] = pick(order[window_to_part], hidden)
     hid = links.halo(r.hid_out, r.hid_in, -1)
-    for copy in cot + hid:
+
+    loads.wait("row_order")
+    for g in range(PARTS):
+        turn(r, 0, g)
+    loads.wait("pos_table", 1)
+    tables(r, 1)
+    for copy in cot:
+        copy.wait_recv()
+    r.grad[...] = pick(order[to_shifted], r.cot_in[...])
+    loads.wait("qkv_weight", 1)
+    loads.wait("proj_weight", 1)
+    for copy in hid:
         copy.wait_recv()
     r.x[1] = pick(order[to_shifted], r.hid_in[...])
-    r.grad[...] = pick(order[to_shifted], r.cot_in[...])
-    forward(r, 1, True)
+    project(r, 1)
+    attention(r, 1)
+    finish_block(r, 1, True)
     backward_norm(r, 1, factor)
     backward_attend(r, 1, 0, GROUPS)
     r.back_out[...] = pick(order[from_shifted], backward_tokens(r, 1))
     back = links.halo(r.back_out, r.back_in, 1)
-    second = [Reduce(r, links, 1, g) for g in range(3)]
-    first = [Reduce(r, links, 0, g) for g in range(3)]
+
     small_part(r, 1, factor)
-    for g in range(3):
+    small_second.advance()
+    for g in range(PARTS):
+        turn(r, 1, g)
         weight_part(r, 1, g, factor)
         second[g].advance()
+    small_second.advance()
+    for job in second:
+        job.advance()
     for copy in back:
         copy.wait_recv()
     r.grad[...] = pick(order[part_to_window], r.back_in[...])
     backward_norm(r, 0, factor)
+    weight_part(r, 0, 3, factor)
+    first[3].advance()
+    backward_attend(r, 0, 0, 2)
+    first[3].advance()
+    small_second.advance()
+    backward_attend(r, 0, 2, 4)
+    small_part(r, 0, factor)
+    small_first.advance()
+    for g in range(3):
+        weight_part(r, 0, g, factor)
+        first[g].advance()
+    small_first.advance()
+    for job in first[:3]:
+        job.advance()
+    small_second.advance()
     for job in second:
         job.advance()
-    for g in range(GROUPS):
-        backward_attend(r, 0, g, g + 1)
-        for job in second:
-            if g < 3:
-                job.advance()
-    small_part(r, 0, factor)
-    weight_part(r, 0, 0, factor)
-    first[0].advance()
-    second[0].advance()
-    for g in (1, 2):
-        weight_part(r, 0, g, factor)
-        first[g].advance()
-    second[0].advance()
     r.d_fields[...] = pick(order[from_window], backward_tokens(r, 0))
-    second[0].advance()
-    for step in range(4):
-        for job in first:
-            job.advance()
-    for step in range(3):
-        first[0].advance()
+    first[3].advance()
+    small_first.advance()
+    for job in first[:3]:
+        job.advance()
+    small_second.advance()
+    for job in second:
+        job.advance()
+    first[3].advance()
+    small_first.advance()
+    for job in first[:3]:
+        job.advance()
+    small_second.advance()
+    for job in second:
+        job.advance()
+    small_first.advance()
+    for job in first:
+        job.advance()
+    small_first.advance()
     links.finish()
+
+
+def deliver(fields, qkv, proj, total, d_fields, d_qkv, d_proj, d_gain, d_log, d_table):
+    d_fields[...] = fields[...]
+    d_qkv[...] = qkv[...]
+    d_proj[...] = proj[...]
+    lane = iota((1, 16), 1)
+    for b in range(2):
+        for k in range(8):
+            at = table_row(k)
+            piece = total[b, at : at + 64, :].astype(F32)
+            d_table[b, 2 * k] = piece[:, 0:64]
+            d_table[b, 2 * k + 1] = piece[:, 64:128]
+        rest = total[b, 256:272, :].astype(F32)
+        for k in range(4):
+            d_gain[b : b + 1, k * 128 : k * 128 + 128] = rest[k : k + 1, :]
+        row = jnp.zeros((1, 16), F32)
+        for h in range(16):
+            spot = rest[8 + h // 2 : 9 + h // 2, h % 2 * 64 : h % 2 * 64 + 1]
+            row = jnp.where(lane == h, spot, row)
+        d_log[b : b + 1, :] = row
 
 
 def local(fields, cotangent, surface, qkv_weight, proj_weight, norm_gain, log_scale, pos_table):
@@ -541,6 +681,7 @@
     shape = jax.ShapeDtypeStruct
     orders = [jnp.asarray(x, BF16) for x in (token_orders(), row_orders())]
     vmem = pl.BlockSpec(memory_space=pltpu.VMEM)
+    any_space = pl.BlockSpec(memory_space=pl.ANY)
     smem = pl.BlockSpec(memory_space=pltpu.SMEM)
 
     def body(*refs):
@@ -548,6 +689,24 @@
 
     out = pl.pallas_call(
         body,
+        out_shape=[
+            shape((TOKENS, WIDTH), BF16),
+            shape((2, 4, 3 * WIDTH), F32),
+            shape((2, 4, WIDTH), F32),
+            shape((2, 2 * HALFROWS, 128), BF16),
+        ],
+        in_specs=[any_space] * 2 + [vmem] + [any_space] * 2 + [vmem, smem] + [any_space] * 3,
+        out_specs=[vmem] * 4,
+        scratch_shapes=list(scratch_spec().values()),
+        compiler_params=pltpu.CompilerParams(
+            collective_id=0, has_side_effects=True, vmem_limit_bytes=60 * 1024 * 1024
+        ),
+    )(
+        fields.reshape(TOKENS, WIDTH), cotangent.reshape(TOKENS, WIDTH), surface, qkv_weight, proj_weight,
+        norm_gain, log_scale, pos_table, *orders,
+    )
+    out = pl.pallas_call(
+        deliver,
         out_shape=[
             shape((TOKENS, WIDTH), BF16),
             shape((2, 4, 3 * WIDTH), F32),
@@ -556,16 +715,9 @@
             shape((2, 16), F32),
             shape((2, 16, 64, 64), F32),
         ],
-        in_specs=[vmem] * 6 + [smem] + [vmem] * 3,
+        in_specs=[vmem] * 4,
         out_specs=[vmem] * 6,
-        scratch_shapes=list(scratch_spec().values()),
-        compiler_params=pltpu.CompilerParams(
-            collective_id=0, has_side_effects=True, vmem_limit_bytes=60 * 1024 * 1024
-        ),
-    )(
-        fields.reshape(TOKENS, WIDTH), cotangent.reshape(TOKENS, WIDTH), surface, qkv_weight, proj_weight,
-        norm_gain, log_scale, pos_table, *orders,
-    )
+    )(*out)
     return (out[0].reshape(LON, LAT, WIDTH),) + tuple(out[1:])
 
 

time: 101 us -> 65.3 us (0.65)
  Pallas kernels: 91.1 us -> 64.5 us
  local copies, waits for them, and re-layouts: 9.23 us -> 0 us
    pallas_call x1, Pallas kernels: 91.1 us -> 62.2 us  [local(): pl.pallas_call(body, out_shape=[shape((TOKENS, WIDTH), BF16), shape((2, 4...]
    unnamed x6 -> x0, local copies, waits for them, and re-layouts: 9.23 us -> none
    pallas_call x0 -> x1, Pallas kernels: none -> 2.25 us  [local(): pl.pallas_call(deliver, out_shape=[shape((TOKENS, WIDTH), BF16), shape((2...]
where the time goes in v2:
time: 65.3 us; the launch traced here: 65.1 us
  Pallas kernels  64.5 us (99%)
    pallas_call x1, Pallas kernels, local(): pl.pallas_call(body, out_shape=[shape((TOKENS, WIDTH), BF16), shape((2, 4...  62.2 us
    pallas_call x1, Pallas kernels, local(): pl.pallas_call(deliver, out_shape=[shape((TOKENS, WIDTH), BF16), shape((2...  2.25 us

profile of v2, /device:TPU:1, one launch (start us, length us, event | category | flops | bytes accessed | tf_op | source)
XLA Modules:
  0.0 65.1 jit_solution(350853785343551480)
XLA Ops:
  0.6 62.2 %shard_map.145 = (bf16[256,512]{1,0:T(8,128)(2,1)}, f32[2,4,1536]{2,1,0:T(4,128)}, f32[2,4,512]{2,1,0:T(4,128)}, bf16[2,576,128]{2,1,0:T(8,128)(2,1)}) custom-call(bf16[256,512]{1,0:T(8,128)(2,1)} %bitcast.3, bf16[256,512]{1,0:T(8,128)(2,1)} %bitcast.4, s32[256,128]{1,0:T(8,128)} %refs_2_.1, bf16[2,512,1536]{2,1,0:T(8,128)(2,1)} %refs_3_.1, ...), custom_call_target="tpu_custom_call" | custom-call | tf_op jit(solution)/shard_map/pallas_call | solution.py:690
  62.8 2.3 %shard_map.146 = (bf16[256,512]{1,0:T(8,128)(2,1)}, f32[2,4,1536]{2,1,0:T(4,128)}, f32[2,4,512]{2,1,0:T(4,128)}, f32[2,512]{1,0:T(2,128)}, f32[2,16]{1,0:T(2,128)}, /*index=5*/f32[2,16,64,64]{3,2,1,0:T(8,128)}) custom-call(bf16[256,512]{1,0:T(8,128)(2,1)} %get-tuple-element.16.fields, f32[2,4,1536]{2,1,0:T(4,128)} %get-tuple-element.17.qkv, ...), custom_call_target="tpu_custom_call" | custom-call | tf_op jit(solution)/shard_map/pallas_call | solution.py:708

commit v3 on v2

--- a/solution.py
+++ b/solution.py
@@ -25,7 +25,7 @@
 MESH = pl.DeviceIdType.MESH
 
 ORDERS = (("x", "y", "z"), ("y", "z", "x"), ("z", "x", "y"))
-ORDER_OF = (0, 1, 2, 2)
+ORDER_OF = ((0, 1, 2, 0), (0, 1, 2, 1))
 
 
 def token_orders():
@@ -89,6 +89,10 @@
     high = x.astype(BF16)
     low = (x - high.astype(F32)).astype(BF16)
     return mm(high, ones) + mm(low, ones)
+
+
+def rough_sum(x, ones):
+    return mm(x.astype(BF16), ones)
 
 
 def scratch_spec():
@@ -115,6 +119,7 @@
         slope=v((2, GROUPS, 64, 256), F32),
         scale=v((2, GROUPS, 1, 256), F32),
         mask=v((2, TOKENS, 256), F32),
+        dcos=v((GROUPS, TOKENS, 256), BF16),
         dtab=v((GROUPS, 64, 256), F32),
         dlog=v((GROUPS, 1, 256), F32),
         hid_out=v((TOKENS, WIDTH), BF16),
@@ -128,14 +133,13 @@
         r1=v((2, PARTS, 256, WIDTH), BF16),
         s1=v((2, PARTS, 256, WIDTH), BF16),
         r2=v((2, PARTS, 3, 64, WIDTH), BF16),
-        s2=v((2, PARTS, 64, WIDTH), BF16),
-        r3=v((2, PARTS, 3, 16, WIDTH), BF16),
-        r4=v((2, PARTS, 4, 16, WIDTH), BF16),
+        s2=v((2, PARTS, 16, 16, 128), BF16),
+        r3=v((2, PARTS, 16, 16, 128), BF16),
         small=v((2, 2 * HALFROWS, 128), BF16),
         small_r1=v((2, HALFROWS, 128), BF16),
         small_x=v((2, 3, 3, 4, PIECE, 128), BF16),
-        send=pltpu.SemaphoreType.DMA((168,)),
-        recv=pltpu.SemaphoreType.DMA((168,)),
+        send=pltpu.SemaphoreType.DMA((224,)),
+        recv=pltpu.SemaphoreType.DMA((224,)),
         load=pltpu.SemaphoreType.DMA((24,)),
         fields_v=v((TOKENS, WIDTH), BF16),
         cotangent_v=v((TOKENS, WIDTH), BF16),
@@ -161,9 +165,11 @@
         self.core = lat % 2
         self.at = dict(x=lon % 4, y=lon // 4 % 4, z=lat // 2 * 2 + lon // 16)
 
-    def along(self, axis, to):
+    def along(self, axis, to, second=None, other=None):
         at = dict(self.at)
         at[axis] = to
+        if second is not None:
+            at[second] = other
         return (at["z"] % 2 * 16 + at["y"] * 4 + at["x"], at["z"] // 2 * 2 + self.core)
 
     def sibling(self):
@@ -177,6 +183,10 @@
         others = [self.sibling()]
         for axis in ("x", "y", "z"):
             others += [self.along(axis, (self.at[axis] + d) % 4) for d in (1, 2, 3)]
+        for a, b in (("x", "y"), ("y", "z"), ("z", "x")):
+            others += [
+                self.along(a, (self.at[a] + i) % 4, b, (self.at[b] + j) % 4) for i in (1, 2, 3) for j in (1, 2, 3)
+            ]
         for d in (-1, 1):
             others += [self.shifted(d, 0), self.shifted(0, d), self.shifted(d, d)]
         for other in others:
@@ -200,6 +210,7 @@
     def finish(self):
         for copy in self.started:
             copy.wait_send()
+        self.started = []
 
     def halo(self, src, dst, sign):
         dst[0:112, :] = src[0:112, :]
@@ -234,7 +245,7 @@
 class Reduce:
     def __init__(self, r, links, b, g):
         self.r, self.links, self.b, self.g = r, links, b, g
-        self.axes = ORDERS[ORDER_OF[g]]
+        self.axes = ORDERS[ORDER_OF[b][g]]
         self.place = [links.at[a] for a in self.axes]
         self.step = 0
 
@@ -263,25 +274,24 @@
             total = r.s1[b, g, rows(self.place[0], 64), :].astype(F32)
             for d in range(3):
                 total += r.r2[b, g, d].astype(F32)
-            r.s2[b, g] = total.astype(BF16)
-            self.waits = [
-                links.send(r.s2.at[b, g, rows(k, 16)], r.r3.at[b, g, d - 1], links.along(self.axes[1], k))
-                for k, d in self.peers(1)
-            ]
+            for chip in range(16):
+                piece = total[4 * chip : 4 * chip + 4, :]
+                piece = jnp.concatenate([piece[:, j * 128 : j * 128 + 128] for j in range(4)], axis=0)
+                r.s2[b, g, chip] = piece.astype(BF16)
+            (_, one, two), (_, i, j) = self.axes, self.place
+            here = i * 4 + j
+            r.r3[b, g, here] = r.s2[b, g, here]
+            self.waits = []
+            for d in range(1, 16):
+                k, m = (i + d // 4) % 4, (j + d % 4) % 4
+                self.waits.append(
+                    links.send(r.s2.at[b, g, k * 4 + m], r.r3.at[b, g, here], links.along(one, k, two, m))
+                )
         elif step == 3:
-            total = r.s2[b, g, rows(self.place[1], 16), :].astype(F32)
-            for d in range(3):
-                total += r.r3[b, g, d].astype(F32)
-            mine = r.r4.at[b, g, self.place[2]]
-            mine[...] = total.astype(BF16)
-            self.waits = [links.send(mine, mine, links.along(self.axes[2], k)) for k, d in self.peers(2)]
-        elif step == 4:
-            total = r.r4[b, g, 0].astype(F32)
-            for k in range(1, 4):
-                total += r.r4[b, g, k].astype(F32)
-            own = total[0:4, :]
-            for k in range(1, 4):
-                own = jnp.where(self.place[2] == k, total[4 * k : 4 * k + 4, :], own)
+            total = r.r3[b, g, 0].astype(F32)
+            for k in range(1, 16):
+                total += r.r3[b, g, k].astype(F32)
+            own = jnp.concatenate([total[4 * j : 4 * j + 4, :] for j in range(4)], axis=1)
             if g == 3:
                 r.d_proj[b] = own
             else:
@@ -407,7 +417,7 @@
     for name, k in (("q", 0), ("k", 1)):
         mixed = mm(x, r.qkv_weight_v[b, :, k * WIDTH : (k + 1) * WIDTH])
         square = mixed * mixed
-        total = jnp.concatenate([run_sum(square[:, o : o + 256], ones32) for o in (0, 256)], axis=1)
+        total = jnp.concatenate([rough_sum(square[:, o : o + 256], ones32) for o in (0, 256)], axis=1)
         inv = lax.rsqrt(total + NORM_EPS)
         unit = mixed * inv
         getattr(r, name + "inv")[b] = inv
@@ -417,7 +427,7 @@
 
 
 def attention(r, b):
-    def attend(g, carry):
+    def attend(g):
         cols = group_lanes(g)
         lanes = head_lanes(BF16)
         ones64 = same_run(256, 64)
@@ -433,9 +443,9 @@
         half = probs.astype(BF16)
         out = [mm(window(half, w), expand(window(v, w), lanes)) for w in range(WINDOWS)]
         r.attended[b, :, cols] = jnp.concatenate(out, axis=0).astype(BF16)
-        return carry
-
-    lax.fori_loop(0, GROUPS, attend, 0)
+
+    for g in range(GROUPS):
+        attend(g)
 
 
 def finish_block(r, b, last):
@@ -467,36 +477,45 @@
     r.datt[...] = mm_nt(dz, r.proj_weight_v[b]).astype(BF16)
 
 
-def backward_attend(r, b, begin, end):
-    def attend(g, carry):
+def backward_values(r, b):
+    wide = head_lanes(F32)
+    for g in range(GROUPS):
         cols = group_lanes(g)
-        lanes, wide = head_lanes(BF16), head_lanes(F32)
-        ones64, ones32 = same_run(256, 64), same_run(128, 32)
-        q, k, v = r.qhalf[b, :, cols], r.khalf[b, :, cols], r.vhalf[b, :, cols]
-        datt = r.datt[:, cols]
-        probs = r.probs[b, g]
-        half = probs.astype(BF16)
+        half, datt = r.probs[b, g].astype(BF16), r.datt[:, cols]
+        dv = [collapse(mm_tn(window(half, w), window(datt, w)), wide) for w in range(WINDOWS)]
+        r.dmixed[:, group_lanes(g, 2 * WIDTH)] = jnp.concatenate(dv, axis=0).astype(BF16)
+
+
+def backward_scores(r, b):
+    lanes = head_lanes(BF16)
+    ones64 = same_run(256, 64)
+    for g in range(GROUPS):
+        cols = group_lanes(g)
+        v, datt, probs = r.vhalf[b, :, cols], r.datt[:, cols], r.probs[b, g]
         dprobs = jnp.concatenate(
             [mm_nt(window(datt, w), expand(window(v, w), lanes)) for w in range(WINDOWS)], axis=0
         )
         dscores = probs * (dprobs - run_sum(probs * dprobs, ones64))
         r.dtab[g] = sum(window(dscores, w) for w in range(WINDOWS))
         r.dlog[g] = jnp.sum(dscores * r.cosine[b, g], axis=0, keepdims=True)
-        dcos = (dscores * r.scale[b, g]).astype(BF16)
-        dq, dk, dv = [], [], []
+        r.dcos[g] = (dscores * r.scale[b, g]).astype(BF16)
+
+
+def backward_keys(r, b, begin, end):
+    lanes, wide = head_lanes(BF16), head_lanes(F32)
+    ones32 = same_run(128, 32)
+    for g in range(begin, end):
+        cols = group_lanes(g)
+        q, k, dcos = r.qhalf[b, :, cols], r.khalf[b, :, cols], r.dcos[g]
+        dq, dk = [], []
         for w in range(WINDOWS):
             dq.append(mm(window(dcos, w), expand(window(k, w), lanes)))
             dk.append(collapse(mm_tn(window(dcos, w), window(q, w)), wide))
-            dv.append(collapse(mm_tn(window(half, w), window(datt, w)), wide))
         for base, parts, unit, inv in ((0, dq, r.qunit, r.qinv), (WIDTH, dk, r.kunit, r.kinv)):
             grad = jnp.concatenate(parts, axis=0)
             unit = unit[b, :, cols]
-            grad = (grad - unit * run_sum(unit * grad, ones32)) * inv[b, :, cols]
+            grad = (grad - unit * rough_sum(unit * grad, ones32)) * inv[b, :, cols]
             r.dmixed[:, group_lanes(g, base)] = grad.astype(BF16)
-        r.dmixed[:, group_lanes(g, 2 * WIDTH)] = jnp.concatenate(dv, axis=0).astype(BF16)
-        return carry
-
-    lax.fori_loop(begin, end, attend, 0)
 
 
 def backward_tokens(r, b):
@@ -521,7 +540,7 @@
 
 def turn(r, b, g):
     left = r.attended if g == 3 else r.x
-    r.turned[b, g] = mm_nt(r.row_order_v[ORDER_OF[g]], left[b]).astype(BF16)
+    r.turned[b, g] = mm_nt(r.row_order_v[ORDER_OF[b][g]], left[b]).astype(BF16)
 
 
 def weight_part(r, b, g, factor):
@@ -564,7 +583,6 @@
     small_second, small_first = SmallSum(r, links, 1), SmallSum(r, links, 0)
 
     masks(r, links, 0)
-    masks(r, links, 1)
     loads.wait("fields")
     loads.wait("token_order")
     r.x[0] = pick(order[to_window], r.fields_v[...])
@@ -573,23 +591,20 @@
     loads.wait("pos_table", 0)
     tables(r, 0)
     attention(r, 0)
+    loads.wait("proj_weight", 0)
+    hidden = finish_block(r, 0, False)
+    r.hid_out[...] = pick(order[window_to_part], hidden)
+    links.met()
+    hid = links.halo(r.hid_out, r.hid_in, -1)
     loads.wait("cotangent")
     r.cot_out[...] = pick(order[to_part], r.cotangent_v[...])
-    loads.wait("proj_weight", 0)
-    links.met()
     cot = links.halo(r.cot_out, r.cot_in, -1)
-    hidden = finish_block(r, 0, False)
-    r.hid_out[...] = pick(order[window_to_part], hidden)
-    hid = links.halo(r.hid_out, r.hid_in, -1)
-
+    masks(r, links, 1)
+    loads.wait("pos_table", 1)
+    tables(r, 1)
     loads.wait("row_order")
     for g in range(PARTS):
         turn(r, 0, g)
-    loads.wait("pos_table", 1)
-    tables(r, 1)
-    for copy in cot:
-        copy.wait_recv()
-    r.grad[...] = pick(order[to_shifted], r.cot_in[...])
     loads.wait("qkv_weight", 1)
     loads.wait("proj_weight", 1)
     for copy in hid:
@@ -598,58 +613,67 @@
     project(r, 1)
     attention(r, 1)
     finish_block(r, 1, True)
+    for copy in cot:
+        copy.wait_recv()
+    r.grad[...] = pick(order[to_shifted], r.cot_in[...])
     backward_norm(r, 1, factor)
-    backward_attend(r, 1, 0, GROUPS)
+    backward_values(r, 1)
+    backward_scores(r, 1)
+    small_part(r, 1, factor)
+    small_second.advance()
+    backward_keys(r, 1, 0, GROUPS)
     r.back_out[...] = pick(order[from_shifted], backward_tokens(r, 1))
     back = links.halo(r.back_out, r.back_in, 1)
 
-    small_part(r, 1, factor)
     small_second.advance()
-    for g in range(PARTS):
+    for g in (3, 2, 1, 0):
         turn(r, 1, g)
         weight_part(r, 1, g, factor)
         second[g].advance()
-    small_second.advance()
-    for job in second:
-        job.advance()
+    for g in (3, 2, 1):
+        second[g].advance()
     for copy in back:
         copy.wait_recv()
+    second[0].advance()
     r.grad[...] = pick(order[part_to_window], r.back_in[...])
     backward_norm(r, 0, factor)
     weight_part(r, 0, 3, factor)
     first[3].advance()
-    backward_attend(r, 0, 0, 2)
+    backward_values(r, 0)
+    weight_part(r, 0, 2, factor)
+    first[2].advance()
     first[3].advance()
-    small_second.advance()
-    backward_attend(r, 0, 2, 4)
+    backward_scores(r, 0)
     small_part(r, 0, factor)
     small_first.advance()
-    for g in range(3):
+    first[2].advance()
+    backward_keys(r, 0, 0, 2)
+    small_first.advance()
+    backward_keys(r, 0, 2, 4)
+    for g in (0, 1):
         weight_part(r, 0, g, factor)
         first[g].advance()
-    small_first.advance()
-    for job in first[:3]:
-        job.advance()
     small_second.advance()
+    first[0].advance()
+    first[1].advance()
     for job in second:
         job.advance()
     r.d_fields[...] = pick(order[from_window], backward_tokens(r, 0))
+    small_first.advance()
+    small_second.advance()
+    first[3].advance()
+    first[2].advance()
+    for job in second:
+        job.advance()
+    small_first.advance()
+    first[0].advance()
+    first[1].advance()
+    small_second.advance()
+    links.finish()
+    small_second.advance()
     first[3].advance()
     small_first.advance()
     for job in first[:3]:
-        job.advance()
-    small_second.advance()
-    for job in second:
-        job.advance()
-    first[3].advance()
-    small_first.advance()
-    for job in first[:3]:
-        job.advance()
-    small_second.advance()
-    for job in second:
-        job.advance()
-    small_first.advance()
-    for job in first:
         job.advance()
     small_first.advance()
     links.finish()

time: 65.3 us -> 62.3 us (0.954)
  Pallas kernels: 64.5 us -> 61.5 us
    pallas_call x1, Pallas kernels: 62.2 us -> 59.3 us  [local(): pl.pallas_call(body, out_shape=[shape((TOKENS, WIDTH), BF16), shape((2, 4...]
where the time goes in v3:
time: 62.3 us; the launch traced here: 62.2 us
  Pallas kernels  61.5 us (99%)
  between operations  0.64 us (1%)
    pallas_call x1, Pallas kernels, local(): pl.pallas_call(body, out_shape=[shape((TOKENS, WIDTH), BF16), shape((2, 4...  59.3 us
    pallas_call x1, Pallas kernels, local(): pl.pallas_call(deliver, out_shape=[shape((TOKENS, WIDTH), BF16), shape((2...  2.25 us

profile of v3, /device:TPU:1, one launch (start us, length us, event | category | flops | bytes accessed | tf_op | source)
XLA Modules:
  0.0 62.2 jit_solution(7345029658536357355)
XLA Ops:
  0.6 59.3 %shard_map.145 = (bf16[256,512]{1,0:T(8,128)(2,1)}, f32[2,4,1536]{2,1,0:T(4,128)}, f32[2,4,512]{2,1,0:T(4,128)}, bf16[2,576,128]{2,1,0:T(8,128)(2,1)}) custom-call(bf16[256,512]{1,0:T(8,128)(2,1)} %bitcast.3, bf16[256,512]{1,0:T(8,128)(2,1)} %bitcast.4, s32[256,128]{1,0:T(8,128)} %refs_2_.1, bf16[2,512,1536]{2,1,0:T(8,128)(2,1)} %refs_3_.1, ...), custom_call_target="tpu_custom_call" | custom-call | tf_op jit(solution)/shard_map/pallas_call | solution.py:714
  59.9 2.3 %shard_map.146 = (bf16[256,512]{1,0:T(8,128)(2,1)}, f32[2,4,1536]{2,1,0:T(4,128)}, f32[2,4,512]{2,1,0:T(4,128)}, f32[2,512]{1,0:T(2,128)}, f32[2,16]{1,0:T(2,128)}, /*index=5*/f32[2,16,64,64]{3,2,1,0:T(8,128)}) custom-call(bf16[256,512]{1,0:T(8,128)(2,1)} %get-tuple-element.16.fields, f32[2,4,1536]{2,1,0:T(4,128)} %get-tuple-element.17.qkv, ...), custom_call_target="tpu_custom_call" | custom-call | tf_op jit(solution)/shard_map/pallas_call | solution.py:732

commit v4 on v3

--- a/solution.py
+++ b/solution.py
@@ -24,6 +24,9 @@
 F32, BF16 = jnp.float32, jnp.bfloat16
 MESH = pl.DeviceIdType.MESH
 
+SPANS = (((0, 48), (112, 48), (224, 16), (240, 16)), ((48, 64), (160, 64)))
+SHIFTED_SPANS = (((0, 64), (112, 64)), ((64, 48), (176, 48), (224, 16), (240, 16)))
+
 ORDERS = (("x", "y", "z"), ("y", "z", "x"), ("z", "x", "y"))
 ORDER_OF = ((0, 1, 2, 0), (0, 1, 2, 1))
 
@@ -36,7 +39,8 @@
     parts = []
     for north in (False, True):
         for west in (False, True):
-            parts += [c for c in cells if (c[0] < HALF) == west and (c[1] < HALF) == north]
+            part = [c for c in cells if (c[0] < HALF) == west and (c[1] < HALF) == north]
+            parts += sorted(part, key=lambda c: ((c[1] >= 16) + (c[1] >= 20), c))
     to_window = np.zeros((TOKENS, TOKENS), np.float32)
     to_part = np.zeros_like(to_window)
     window_to_part = np.zeros_like(to_window)
@@ -212,13 +216,15 @@
             copy.wait_send()
         self.started = []
 
-    def halo(self, src, dst, sign):
-        dst[0:112, :] = src[0:112, :]
-        spans = ((112, 112, (sign, 0)), (224, 16, (0, sign)), (240, 16, (sign, sign)))
-        return [
-            self.send(src.at[pl.ds(o, n)], dst.at[pl.ds(o, n)], self.shifted(*to))
-            for o, n, to in spans
-        ]
+    def halo(self, src, dst, sign, spans):
+        copies = []
+        for first, count in spans:
+            if first < 112:
+                dst[first : first + count, :] = src[first : first + count, :]
+                continue
+            to = (sign, 0) if first < 224 else ((0, sign) if first < 240 else (sign, sign))
+            copies.append(self.send(src.at[pl.ds(first, count)], dst.at[pl.ds(first, count)], self.shifted(*to)))
+        return copies
 
 
 class Loads:
@@ -417,7 +423,7 @@
     for name, k in (("q", 0), ("k", 1)):
         mixed = mm(x, r.qkv_weight_v[b, :, k * WIDTH : (k + 1) * WIDTH])
         square = mixed * mixed
-        total = jnp.concatenate([rough_sum(square[:, o : o + 256], ones32) for o in (0, 256)], axis=1)
+        total = jnp.concatenate([run_sum(square[:, o : o + 256], ones32) for o in (0, 256)], axis=1)
         inv = lax.rsqrt(total + NORM_EPS)
         unit = mixed * inv
         getattr(r, name + "inv")[b] = inv
@@ -426,38 +432,41 @@
     r.vhalf[b] = mm(x, r.qkv_weight_v[b, :, 2 * WIDTH : 3 * WIDTH]).astype(BF16)
 
 
-def attention(r, b):
+def attention(r, b, begin=0, end=WINDOWS):
+    tokens = slice(begin * 64, end * 64)
+    count = end - begin
+
     def attend(g):
         cols = group_lanes(g)
         lanes = head_lanes(BF16)
         ones64 = same_run(256, 64)
-        q, k, v = r.qhalf[b, :, cols], r.khalf[b, :, cols], r.vhalf[b, :, cols]
+        q, k, v = r.qhalf[b, tokens, cols], r.khalf[b, tokens, cols], r.vhalf[b, tokens, cols]
         cosine = jnp.concatenate(
-            [mm_nt(window(q, w), expand(window(k, w), lanes)) for w in range(WINDOWS)], axis=0
+            [mm_nt(window(q, w), expand(window(k, w), lanes)) for w in range(count)], axis=0
         )
-        r.cosine[b, g] = cosine
-        bias = jnp.concatenate([r.bias[b, g]] * WINDOWS, axis=0)
-        expo = jnp.exp(cosine * r.scale[b, g] + bias) * r.mask[b]
+        r.cosine[b, g, tokens, :] = cosine
+        bias = jnp.concatenate([r.bias[b, g]] * count, axis=0)
+        expo = jnp.exp(cosine * r.scale[b, g] + bias) * r.mask[b, tokens, :]
         probs = expo / run_sum(expo, ones64)
-        r.probs[b, g] = probs
+        r.probs[b, g, tokens, :] = probs
         half = probs.astype(BF16)
-        out = [mm(window(half, w), expand(window(v, w), lanes)) for w in range(WINDOWS)]
-        r.attended[b, :, cols] = jnp.concatenate(out, axis=0).astype(BF16)
+        out = [mm(window(half, w), expand(window(v, w), lanes)) for w in range(count)]
+        r.attended[b, tokens, cols] = jnp.concatenate(out, axis=0).astype(BF16)
 
     for g in range(GROUPS):
         attend(g)
 
 
-def finish_block(r, b, last):
-    z = mm(r.attended[b], r.proj_weight_v[b])
+def finish_block(r, b, tokens):
+    z = mm(r.attended[b, tokens, :], r.proj_weight_v[b])
     centred = z - jnp.mean(z, axis=-1, keepdims=True)
     inverse = lax.rsqrt(jnp.mean(centred * centred, axis=-1, keepdims=True) + LAYER_EPS)
     normed = centred * inverse
-    r.inverse[b] = inverse
-    r.normed[b] = normed
-    if last:
+    r.inverse[b, tokens, :] = inverse
+    r.normed[b, tokens, :] = normed
+    if b == 1:
         return None
-    return (r.x[b].astype(F32) + normed * r.norm_gain[b : b + 1, :]).astype(BF16)
+    return (r.x[b, tokens, :].astype(F32) + normed * r.norm_gain[b : b + 1, :]).astype(BF16)
 
 
 def backward_norm(r, b, factor):
@@ -501,25 +510,26 @@
         r.dcos[g] = (dscores * r.scale[b, g]).astype(BF16)
 
 
-def backward_keys(r, b, begin, end):
+def backward_keys(r, b, begin, end, first, last):
+    tokens = slice(first * 64, last * 64)
     lanes, wide = head_lanes(BF16), head_lanes(F32)
     ones32 = same_run(128, 32)
     for g in range(begin, end):
         cols = group_lanes(g)
-        q, k, dcos = r.qhalf[b, :, cols], r.khalf[b, :, cols], r.dcos[g]
+        q, k, dcos = r.qhalf[b, tokens, cols], r.khalf[b, tokens, cols], r.dcos[g, tokens, :]
         dq, dk = [], []
-        for w in range(WINDOWS):
+        for w in range(last - first):
             dq.append(mm(window(dcos, w), expand(window(k, w), lanes)))
             dk.append(collapse(mm_tn(window(dcos, w), window(q, w)), wide))
         for base, parts, unit, inv in ((0, dq, r.qunit, r.qinv), (WIDTH, dk, r.kunit, r.kinv)):
             grad = jnp.concatenate(parts, axis=0)
-            unit = unit[b, :, cols]
-            grad = (grad - unit * rough_sum(unit * grad, ones32)) * inv[b, :, cols]
-            r.dmixed[:, group_lanes(g, base)] = grad.astype(BF16)
-
-
-def backward_tokens(r, b):
-    grad = r.grad[...].astype(F32) + mm_nt(r.dmixed[...], r.qkv_weight_v[b])
+            unit = unit[b, tokens, cols]
+            grad = (grad - unit * rough_sum(unit * grad, ones32)) * inv[b, tokens, cols]
+            r.dmixed[tokens, group_lanes(g, base)] = grad.astype(BF16)
+
+
+def backward_tokens(r, b, tokens=slice(0, TOKENS)):
+    grad = r.grad[tokens, :].astype(F32) + mm_nt(r.dmixed[tokens, :], r.qkv_weight_v[b])
     return grad.astype(BF16)
 
 
@@ -590,15 +600,20 @@
     project(r, 0)
     loads.wait("pos_table", 0)
     tables(r, 0)
+    loads.wait("proj_weight", 0)
+    hid = []
     attention(r, 0)
-    loads.wait("proj_weight", 0)
-    hidden = finish_block(r, 0, False)
-    r.hid_out[...] = pick(order[window_to_part], hidden)
-    links.met()
-    hid = links.halo(r.hid_out, r.hid_in, -1)
+    for k in range(2):
+        tokens = slice(k * 128, k * 128 + 128)
+        hidden = finish_block(r, 0, tokens)
+        for at, count in SPANS[k]:
+            r.hid_out[at : at + count, :] = pick(order[window_to_part, at : at + count, tokens], hidden)
+        if k == 0:
+            links.met()
+        hid += links.halo(r.hid_out, r.hid_in, -1, SPANS[k])
     loads.wait("cotangent")
     r.cot_out[...] = pick(order[to_part], r.cotangent_v[...])
-    cot = links.halo(r.cot_out, r.cot_in, -1)
+    cot = links.halo(r.cot_out, r.cot_in, -1, SPANS[0] + SPANS[1])
     masks(r, links, 1)
     loads.wait("pos_table", 1)
     tables(r, 1)
@@ -612,7 +627,7 @@
     r.x[1] = pick(order[to_shifted], r.hid_in[...])
     project(r, 1)
     attention(r, 1)
-    finish_block(r, 1, True)
+    finish_block(r, 1, slice(0, TOKENS))
     for copy in cot:
         copy.wait_recv()
     r.grad[...] = pick(order[to_shifted], r.cot_in[...])
@@ -621,9 +636,14 @@
     backward_scores(r, 1)
     small_part(r, 1, factor)
     small_second.advance()
-    backward_keys(r, 1, 0, GROUPS)
-    r.back_out[...] = pick(order[from_shifted], backward_tokens(r, 1))
-    back = links.halo(r.back_out, r.back_in, 1)
+    back = []
+    backward_keys(r, 1, 0, GROUPS, 0, WINDOWS)
+    for k in range(2):
+        tokens = slice(k * 128, k * 128 + 128)
+        grad = backward_tokens(r, 1, tokens)
+        for at, count in SHIFTED_SPANS[k]:
+            r.back_out[at : at + count, :] = pick(order[from_shifted, at : at + count, tokens], grad)
+        back += links.halo(r.back_out, r.back_in, 1, SHIFTED_SPANS[k])
 
     small_second.advance()
     for g in (3, 2, 1, 0):
@@ -637,6 +657,7 @@
     second[0].advance()
     r.grad[...] = pick(order[part_to_window], r.back_in[...])
     backward_norm(r, 0, factor)
+    small_second.advance()
     weight_part(r, 0, 3, factor)
     first[3].advance()
     backward_values(r, 0)
@@ -647,34 +668,35 @@
     small_part(r, 0, factor)
     small_first.advance()
     first[2].advance()
-    backward_keys(r, 0, 0, 2)
+    backward_keys(r, 0, 0, 2, 0, WINDOWS)
     small_first.advance()
-    backward_keys(r, 0, 2, 4)
-    for g in (0, 1):
-        weight_part(r, 0, g, factor)
-        first[g].advance()
-    small_second.advance()
+    backward_keys(r, 0, 2, 4, 0, WINDOWS)
+    weight_part(r, 0, 0, factor)
+    first[0].advance()
+    weight_part(r, 0, 1, factor)
+    first[1].advance()
     first[0].advance()
     first[1].advance()
-    for job in second:
-        job.advance()
+    small_second.advance()
     r.d_fields[...] = pick(order[from_window], backward_tokens(r, 0))
     small_first.advance()
-    small_second.advance()
     first[3].advance()
     first[2].advance()
     for job in second:
         job.advance()
+    small_second.advance()
     small_first.advance()
     first[0].advance()
     first[1].advance()
-    small_second.advance()
     links.finish()
     small_second.advance()
+    for job in second:
+        job.advance()
     first[3].advance()
     small_first.advance()
-    for job in first[:3]:
-        job.advance()
+    first[0].advance()
+    first[1].advance()
+    first[2].advance()
     small_first.advance()
     links.finish()
 

time: 62.3 us -> 60.6 us (0.973)
  Pallas kernels: 61.5 us -> 59.8 us
    pallas_call x1, Pallas kernels: 59.3 us -> 57.5 us  [local(): pl.pallas_call(body, out_shape=[shape((TOKENS, WIDTH), BF16), shape((2, 4...]
where the time goes in v4:
time: 60.6 us; the launch traced here: 60.4 us
  Pallas kernels  59.8 us (99%)
  between operations  0.64 us (1%)
    pallas_call x1, Pallas kernels, local(): pl.pallas_call(body, out_shape=[shape((TOKENS, WIDTH), BF16), shape((2, 4...  57.5 us
    pallas_call x1, Pallas kernels, local(): pl.pallas_call(deliver, out_shape=[shape((TOKENS, WIDTH), BF16), shape((2...  2.25 us

profile of v4, /device:TPU:1, one launch (start us, length us, event | category | flops | bytes accessed | tf_op | source)
XLA Modules:
  0.0 60.4 jit_solution(4561851548533145815)
XLA Ops:
  0.6 57.5 %shard_map.145 = (bf16[256,512]{1,0:T(8,128)(2,1)}, f32[2,4,1536]{2,1,0:T(4,128)}, f32[2,4,512]{2,1,0:T(4,128)}, bf16[2,576,128]{2,1,0:T(8,128)(2,1)}) custom-call(bf16[256,512]{1,0:T(8,128)(2,1)} %bitcast.3, bf16[256,512]{1,0:T(8,128)(2,1)} %bitcast.4, s32[256,128]{1,0:T(8,128)} %refs_2_.1, bf16[2,512,1536]{2,1,0:T(8,128)(2,1)} %refs_3_.1, ...), custom_call_target="tpu_custom_call" | custom-call | tf_op jit(solution)/shard_map/pallas_call | solution.py:736
  58.2 2.3 %shard_map.146 = (bf16[256,512]{1,0:T(8,128)(2,1)}, f32[2,4,1536]{2,1,0:T(4,128)}, f32[2,4,512]{2,1,0:T(4,128)}, f32[2,512]{1,0:T(2,128)}, f32[2,16]{1,0:T(2,128)}, /*index=5*/f32[2,16,64,64]{3,2,1,0:T(8,128)}) custom-call(bf16[256,512]{1,0:T(8,128)(2,1)} %get-tuple-element.16.fields, f32[2,4,1536]{2,1,0:T(4,128)} %get-tuple-element.17.qkv, ...), custom_call_target="tpu_custom_call" | custom-call | tf_op jit(solution)/shard_map/pallas_call | solution.py:754

commit v5 on v4

--- a/solution.py
+++ b/solution.py
@@ -23,6 +23,8 @@
 CAP = 16.0
 F32, BF16 = jnp.float32, jnp.bfloat16
 MESH = pl.DeviceIdType.MESH
+
+FAR_FIRST = (10, 6, 14, 9, 11, 2, 8, 5, 7, 13, 15, 1, 3, 4, 12)
 
 SPANS = (((0, 48), (112, 48), (224, 16), (240, 16)), ((48, 64), (160, 64)))
 SHIFTED_SPANS = (((0, 64), (112, 64)), ((64, 48), (176, 48), (224, 16), (240, 16)))
@@ -257,7 +259,7 @@
 
     def peers(self, level):
         axis, place = self.axes[level], self.place[level]
-        return [((place + d) % 4, d) for d in (1, 2, 3)]
+        return [((place + d) % 4, d) for d in (2, 1, 3)]
 
     def advance(self):
         r, links, b, g = self.r, self.links, self.b, self.g
@@ -288,7 +290,7 @@
             here = i * 4 + j
             r.r3[b, g, here] = r.s2[b, g, here]
             self.waits = []
-            for d in range(1, 16):
+            for d in FAR_FIRST:
                 k, m = (i + d // 4) % 4, (j + d % 4) % 4
                 self.waits.append(
                     links.send(r.s2.at[b, g, k * 4 + m], r.r3.at[b, g, here], links.along(one, k, two, m))
@@ -314,7 +316,7 @@
         axis = ORDERS[piece][level]
         place = links.at[axis]
         mine = r.small_x.at[b, level, piece, place]
-        return [links.send(mine, mine, links.along(axis, (place + d) % 4)) for d in (1, 2, 3)]
+        return [links.send(mine, mine, links.along(axis, (place + d) % 4)) for d in (2, 1, 3)]
 
     def advance(self):
         r, links, b = self.r, self.links, self.b

time: 60.6 us -> 60 us (0.990)
  no operation moved by 1% of the time
where the time goes in v5:
time: 60 us; the launch traced here: 59.8 us
  Pallas kernels  59.2 us (99%)
  between operations  0.64 us (1%)
    pallas_call x1, Pallas kernels, local(): pl.pallas_call(body, out_shape=[shape((TOKENS, WIDTH), BF16), shape((2, 4...  56.9 us
    pallas_call x1, Pallas kernels, local(): pl.pallas_call(deliver, out_shape=[shape((TOKENS, WIDTH), BF16), shape((2...  2.25 us

profile of v5, /device:TPU:1, one launch (start us, length us, event | category | flops | bytes accessed | tf_op | source)
XLA Modules:
  0.0 59.8 jit_solution(6200342883643700299)
XLA Ops:
  0.6 56.9 %shard_map.145 = (bf16[256,512]{1,0:T(8,128)(2,1)}, f32[2,4,1536]{2,1,0:T(4,128)}, f32[2,4,512]{2,1,0:T(4,128)}, bf16[2,576,128]{2,1,0:T(8,128)(2,1)}) custom-call(bf16[256,512]{1,0:T(8,128)(2,1)} %bitcast.3, bf16[256,512]{1,0:T(8,128)(2,1)} %bitcast.4, s32[256,128]{1,0:T(8,128)} %refs_2_.1, bf16[2,512,1536]{2,1,0:T(8,128)(2,1)} %refs_3_.1, ...), custom_call_target="tpu_custom_call" | custom-call | tf_op jit(solution)/shard_map/pallas_call | solution.py:738
  57.6 2.3 %shard_map.146 = (bf16[256,512]{1,0:T(8,128)(2,1)}, f32[2,4,1536]{2,1,0:T(4,128)}, f32[2,4,512]{2,1,0:T(4,128)}, f32[2,512]{1,0:T(2,128)}, f32[2,16]{1,0:T(2,128)}, /*index=5*/f32[2,16,64,64]{3,2,1,0:T(8,128)}) custom-call(bf16[256,512]{1,0:T(8,128)(2,1)} %get-tuple-element.16.fields, f32[2,4,1536]{2,1,0:T(4,128)} %get-tuple-element.17.qkv, ...), custom_call_target="tpu_custom_call" | custom-call | tf_op jit(solution)/shard_map/pallas_call | solution.py:756
